TPU v7x, 512 devices: a whole 4x8x8 slice. The times are simulated.
512 devices in a mesh: dp: 32 (over y_lo, x, core), mp: 16 (over z, y_hi).
Axes of the slice: x: 4, y: 8 (y_hi: 2, y_lo: 4; y = y_hi * 4 + y_lo), z: 8, core: 2. Of those that a mesh axis runs over, the one named last changes fastest.
Arguments:
- query_rows: bfloat16 [8192, 4096], P('dp', 'mp'), may hold values from -8.5 to 8.5
- key_rows: bfloat16 [8192, 4096], P('dp', 'mp'), may hold values from -8.5 to 8.5
- value_rows: bfloat16 [8192, 4096], P('dp', 'mp'), may hold values from -12 to 12
- out_weight: bfloat16 [4096, 6144], P('mp', 'dp'), may hold values from -0.1875 to 0.1875
- grad_out: bfloat16 [8192, 6144], P('dp', 'mp'), may hold values from -6 to 6
Outputs:
- layer_out: bfloat16 [8192, 6144], P('dp', 'mp')
- grad_query: bfloat16 [8192, 4096], P('dp', 'mp')
- grad_key: bfloat16 [8192, 4096], P('dp', 'mp')
- grad_value: bfloat16 [8192, 4096], P('dp', 'mp')
- grad_weight: float32 [4096, 6144], P('mp', 'dp')
All inputs are finite; a program needn't handle non-finite values.
Results may differ from a plain program's by a relative error of at most 0.019.
Values may be sent and summed in bfloat16 or wider, within the bound.
No kernel may reach another device: no remote copies, remote signals or barrier semaphores. Data moves between devices by JAX's collectives and lax.ppermute only.
A program may use at most 64 MiB of HBM per device.

v0:
```python
import math

import jax
import jax.numpy as jnp
from jax import lax
from jax.sharding import PartitionSpec as P

HEAD = 128
PATCHES = 256


def local(query_rows, key_rows, value_rows, out_weight, grad_out):
    row_count = query_rows.shape[0]
    col_count = query_rows.shape[1]
    heads_here = col_count // HEAD
    images = row_count // PATCHES
    factor = 1.0 / math.sqrt(HEAD)
    shaped = (images, PATCHES, heads_here, HEAD)
    query_four = query_rows.reshape(shaped)
    key_four = key_rows.reshape(shaped)
    value_four = value_rows.reshape(shaped)
    scores = (
        jnp.einsum("bqhd,bkhd->bhqk", query_four, key_four, preferred_element_type=jnp.float32)
        * factor
    )
    maximum = jnp.max(scores, axis=-1, keepdims=True)
    exponent = jnp.exp(scores - maximum)
    probs = exponent / jnp.sum(exponent, axis=-1, keepdims=True)
    probs_low = probs.astype(jnp.bfloat16)
    context = jnp.einsum(
        "bhqk,bkhd->bqhd", probs_low, value_four, preferred_element_type=jnp.float32
    )
    context = context.astype(jnp.bfloat16).reshape(row_count, col_count)
    full_weight = lax.all_gather(out_weight, "dp", axis=1, tiled=True)
    partial_out = jnp.dot(context, full_weight, preferred_element_type=jnp.float32)
    layer_out = lax.psum_scatter(
        partial_out.astype(jnp.bfloat16), "mp", scatter_dimension=1, tiled=True
    )
    cotangent = lax.all_gather(grad_out, "mp", axis=1, tiled=True)
    dcontext = lax.dot_general(
        cotangent, full_weight, (((1,), (1,)), ((), ())), preferred_element_type=jnp.float32
    )
    dcontext_low = dcontext.astype(jnp.bfloat16)
    local_grad = lax.dot_general(
        context, cotangent, (((0,), (0,)), ((), ())), preferred_element_type=jnp.float32
    ).astype(jnp.bfloat16)
    received = lax.all_to_all(local_grad, "dp", split_axis=1, concat_axis=0, tiled=True)
    grad_weight = received.reshape(-1, col_count, received.shape[1]).astype(jnp.float32).sum(axis=0)
    dctx_four = dcontext_low.reshape(shaped)
    grad_value = jnp.einsum(
        "bhqk,bqhd->bkhd", probs_low, dctx_four, preferred_element_type=jnp.float32
    )
    dprobs = jnp.einsum(
        "bqhd,bkhd->bhqk", dctx_four, value_four, preferred_element_type=jnp.float32
    )
    center = jnp.sum(probs * dprobs, axis=-1, keepdims=True)
    dscores = (probs * (dprobs - center)).astype(jnp.bfloat16)
    grad_query = (
        jnp.einsum("bhqk,bkhd->bqhd", dscores, key_four, preferred_element_type=jnp.float32)
        * factor
    )
    grad_key = (
        jnp.einsum("bhqk,bqhd->bkhd", dscores, query_four, preferred_element_type=jnp.float32)
        * factor
    )
    grad_query = grad_query.astype(jnp.bfloat16).reshape(row_count, col_count)
    grad_key = grad_key.astype(jnp.bfloat16).reshape(row_count, col_count)
    grad_value = grad_value.astype(jnp.bfloat16).reshape(row_count, col_count)
    return (layer_out, grad_query, grad_key, grad_value, grad_weight)


def solution(mesh):
    in_specs = (P("dp", "mp"), P("dp", "mp"), P("dp", "mp"), P("mp", "dp"), P("dp", "mp"))
    out_specs = (P("dp", "mp"), P("dp", "mp"), P("dp", "mp"), P("dp", "mp"), P("mp", "dp"))
    return jax.shard_map(local, mesh=mesh, in_specs=in_specs, out_specs=out_specs, check_vma=False)
```

profile of v0, /device:TPU:56, one launch (start us, length us, event | category | flops | bytes accessed | tf_op | source)
XLA Modules:
  0.0 471.0 jit_solution(8185829827889939741)
XLA Ops:
  7.2 0.0 copy-start
  7.2 0.0 all-gather.5.cloned.1.call-start
  7.2 0.7 all-gather.5.cloned.1.call-update
  7.9 0.0 all-gather.3.cloned.1.call-start
  8.0 0.7 all-gather.3.cloned.1.call-update
  8.7 1.0 copy.61
  9.7 0.0 copy-start.2
  9.7 1.1 copy.62
  10.7 0.0 copy-start.3
  10.8 1.2 fusion.14
  11.9 0.0 copy-done
  11.9 0.5 convolution_convert_fusion.2
  12.5 116.7 %all-gather.5.cloned.1.call-done = bf16[256,6144]{1,0:T(8,128)(2,1)} async-done(((bf16[256,384]{1,0:T(8,128)(2,1)}), bf16[256,6144]{1,0:T(8,128)(2,1)}) %all-gather.5.cloned.1.call-update) | async-done | bytes 3145744 | tf_op jit(solution)/shard_map/all_gather | solution.py:39
  129.2 0.0 copy-done.2
  129.2 0.0 copy-done.3
  129.2 2.9 convolution_convert_fusion
  132.1 2.8 copy.50
  134.9 13.2 %all-to-all-start = ((bf16[256,32,192]{0,2,1:T(8,128)(2,1)}), bf16[256,32,192]{0,2,1:T(8,128)(2,1)S(1)}, u32[]{:S(2)}, u32[]{:S(2)}) async-start(bf16[256,32,192]{0,2,1:T(8,128)(2,1)} %bitcast.64), calls=%async_computation | async-start | bytes 6291456 | tf_op jit(solution)/shard_map/all_to_all | solution.py:47
  148.1 0.0 reduce-scatter.4.cloned.1.call-start
  148.2 82.2 %all-gather.3.cloned.1.call-done = bf16[256,6144]{0,1:T(8,128)(2,1)} async-done(((bf16[256,192]{0,1:T(8,128)(2,1)}), bf16[256,6144]{0,1:T(8,128)(2,1)}) %all-gather.3.cloned.1.call-update) | async-done | bytes 3145744 | tf_op jit(solution)/shard_map/all_gather | solution.py:34
  230.4 4.6 convolution_convert_fusion.1
  235.0 4.7 copy.59
  239.7 0.0 reduce-scatter.4.cloned.1.call-update
  239.7 0.0 copy-start.1
  239.7 4.2 convolution_convert_fusion.4
  244.0 0.0 copy-start.5
  244.0 0.0 copy-start.4
  244.0 0.0 copy-done.1
  244.0 0.2 multiply_reduce_fusion
  244.2 0.1 multiply_convert_fusion
  244.3 0.6 copy-done.4
  244.9 0.8 fusion.4
  245.8 0.0 copy-done.5
  245.8 1.7 copy.51
  247.4 1.8 fusion.3
  249.2 1.7 copy.52
  250.9 1.6 convolution_convert_fusion.3
  252.5 0.8 copy.53
  253.3 0.0 all-to-all-done
  253.3 1.1 convert_reduce_fusion
  254.4 208.4 %reduce-scatter.4.cloned.1.call-done = bf16[384,256]{1,0:T(8,128)(2,1)} async-done(((bf16[6144,256]{1,0:T(8,128)(2,1)}), bf16[384,256]{1,0:T(8,128)(2,1)}) %reduce-scatter.4.cloned.1.call-update) | async-done | bytes 196624
  462.8 1.7 copy.60
Async XLA Ops:
  7.2 4.8 %copy-start = (bf16[256,256]{1,0:T(8,128)(2,1)S(1)}, bf16[256,256]{1,0:T(8,128)(2,1)}, u32[]{:S(2)}) copy-start(bf16[256,256]{1,0:T(8,128)(2,1)} %param.7) | copy-start | bytes 393220
  7.2 122.0 %all-gather.5.cloned.1.call-start = ((), (), s32[]{:S(2)}) async-start(), calls=%async_computation.3 | async-start | bytes 3342336 | tf_op jit(solution)/shard_map/all_gather | solution.py:39
  7.9 222.5 %all-gather.3.cloned.1.call-start = ((), (), s32[]{:S(2)}) async-start(), calls=%async_computation.2 | async-start | bytes 3244032 | tf_op jit(solution)/shard_map/all_gather | solution.py:34
  9.7 119.5 %copy-start.2 = (bf16[256,256]{0,1:T(8,128)(2,1)}, bf16[256,256]{0,1:T(8,128)(2,1)S(1)}, u32[]{:S(2)}) copy-start(bf16[256,256]{0,1:T(8,128)(2,1)S(1)} %copy.61) | copy-start | bytes 393220
  10.7 118.5 %copy-start.3 = (bf16[256,256]{0,1:T(8,128)(2,1)}, bf16[256,256]{0,1:T(8,128)(2,1)S(1)}, u32[]{:S(2)}) copy-start(bf16[256,256]{0,1:T(8,128)(2,1)S(1)} %copy.62) | copy-start | bytes 393220
  134.9 118.4 %all-to-all-start = ((bf16[256,32,192]{0,2,1:T(8,128)(2,1)}), bf16[256,32,192]{0,2,1:T(8,128)(2,1)S(1)}, u32[]{:S(2)}, u32[]{:S(2)}) async-start(bf16[256,32,192]{0,2,1:T(8,128)(2,1)} %bitcast.64), calls=%async_computation | async-start | bytes 6291456 | tf_op jit(solution)/shard_map/all_to_all | solution.py:47
  148.1 314.6 %reduce-scatter.4.cloned.1.call-start = ((), (), s32[]{:S(2)}) async-start(), calls=%async_computation.4 | async-start | bytes 3342336
  239.7 4.3 copy-start.1
  244.0 1.8 copy-start.5
  244.0 1.0 copy-start.4
Sparse Core Ops, SparseCore 0:
  11.1 118.0 all-gather.4
  131.3 99.0 all-gather.2
  239.8 222.8 reduce-scatter.3
where the time goes:
time: 475 us; the launch traced here: 471 us
  waiting for transfers between devices  409 us (86%)
  matrix products  17.9 us (4%)
  local copies, waits for them, and re-layouts  16 us (3%)
  between operations  13.9 us (3%)
  starting transfers between devices  13.4 us (3%)
    unnamed x4, waiting for transfers between devices  210 us
    all_gather x1, waiting for transfers between devices, local(): cotangent = lax.all_gather(grad_out, 'mp', axis=1, tiled=True)  117 us
    all_gather x1, waiting for transfers between devices, local(): full_weight = lax.all_gather(out_weight, 'dp', axis=1, tiled=True)  82.2 us
    all_to_all x1, starting transfers between devices, local(): lax.all_to_all(local_grad, 'dp', split_axis=1, concat_axis=0, tiled=True)  13.2 us
    unnamed x17, local copies, waits for them, and re-layouts  11.2 us
  transfers between devices with their start and end apart: 4, of which 3 were waited for; matrix products, arithmetic and copies ran while one was open for 7% of the time, Pallas kernels for 0%

commit v1 on v0

v1 whole, which is shorter than its diff:
```python
import math

import jax
import jax.numpy as jnp
from jax import lax
from jax.sharding import Mesh, PartitionSpec as P

HEAD = 128
PATCHES = 256
AXES = ("y_lo", "x", "core", "z_hi", "z_lo", "y_hi")
SIZES = (4, 4, 2, 4, 2, 2)
ROWS = ("y_lo", "x", "core")
COLS = ("z_hi", "z_lo", "y_hi")
BF16 = jnp.bfloat16
F32 = jnp.float32


def swap_pairs():
    return [(p * 4 + q, q * 4 + p) for p in range(4) for q in range(4)]


def gather(block, axis, count):
    wide = jnp.broadcast_to(block[None], (count,) + block.shape)
    return lax.all_to_all(wide, axis, split_axis=0, concat_axis=0, tiled=True)


def scatter(blocks, axis):
    return lax.all_to_all(blocks, axis, split_axis=0, concat_axis=0, tiled=True)


def total(blocks):
    return blocks.astype(F32).sum(axis=0)


def other_core(block):
    return lax.ppermute(block, "core", [(0, 1), (1, 0)])


def local(query_rows, key_rows, value_rows, out_weight, grad_out):
    factor = 1.0 / math.sqrt(HEAD)
    core = lax.axis_index("core")

    weight = lax.ppermute(out_weight.T, ("y_lo", "z_hi"), swap_pairs())
    weight = gather(weight, "y_lo", 4)
    weight = gather(weight, "x", 4)
    far = other_core(weight)
    first = jnp.where(core == 0, weight, far)
    second = jnp.where(core == 0, far, weight)
    weight = jnp.stack([first, second], axis=2)
    weight = weight.reshape(4, 4, 384, 256)

    cot = gather(grad_out, ("z_lo", "y_hi"), 4)

    heads = lambda v: v.reshape(PATCHES, 2, HEAD)
    query, key, value = heads(query_rows), heads(key_rows), heads(value_rows)
    scores = jnp.einsum("qhd,khd->hqk", query, key, preferred_element_type=F32) * factor
    maximum = jnp.max(scores, axis=-1, keepdims=True)
    exponent = jnp.exp(scores - maximum)
    probs = exponent / jnp.sum(exponent, axis=-1, keepdims=True)
    probs_low = probs.astype(BF16)
    context = jnp.einsum("hqk,khd->qhd", probs_low, value, preferred_element_type=F32)
    context = context.astype(BF16).reshape(PATCHES, 2 * HEAD)
    ctx = gather(context, "z_hi", 4)

    term = jnp.einsum("xrn,ark->xank", cot, ctx, preferred_element_type=F32).astype(BF16)
    term = term.reshape(4, 4, 2, 192, 256)
    mine = jnp.where(core == 0, term[:, :, 0], term[:, :, 1])
    theirs = jnp.where(core == 0, term[:, :, 1], term[:, :, 0])
    term = (mine.astype(F32) + other_core(theirs).astype(F32)).astype(BF16)
    term = total(scatter(term, "x")).astype(BF16)
    term = total(scatter(term, "y_lo")).astype(BF16)
    term = lax.ppermute(term, ("y_lo", "z_hi"), swap_pairs())
    grad_weight = term.T.astype(F32)

    dctx = jnp.einsum("xrn,xank->ark", cot, weight, preferred_element_type=F32).astype(BF16)
    dctx = total(scatter(dctx, "z_hi")).astype(BF16)
    out = jnp.einsum("ark,xank->xrn", ctx, weight, preferred_element_type=F32).astype(BF16)
    layer_out = total(scatter(out, ("z_lo", "y_hi"))).astype(BF16)

    dctx = heads(dctx)
    grad_value = jnp.einsum("hqk,qhd->khd", probs_low, dctx, preferred_element_type=F32)
    dprobs = jnp.einsum("qhd,khd->hqk", dctx, value, preferred_element_type=F32)
    center = jnp.sum(probs * dprobs, axis=-1, keepdims=True)
    dscores = (probs * (dprobs - center)).astype(BF16)
    grad_query = jnp.einsum("hqk,khd->qhd", dscores, key, preferred_element_type=F32) * factor
    grad_key = jnp.einsum("hqk,qhd->khd", dscores, query, preferred_element_type=F32) * factor
    flat = lambda v: v.astype(BF16).reshape(PATCHES, 2 * HEAD)
    return (layer_out, flat(grad_query), flat(grad_key), flat(grad_value), grad_weight)


def solution(mesh):
    fine = Mesh(mesh.devices.reshape(SIZES), AXES)
    rows_cols, cols_rows = P(ROWS, COLS), P(COLS, ROWS)
    in_specs = (rows_cols, rows_cols, rows_cols, cols_rows, rows_cols)
    out_specs = (rows_cols, rows_cols, rows_cols, rows_cols, cols_rows)
    return jax.shard_map(local, mesh=fine, in_specs=in_specs, out_specs=out_specs, check_vma=False)
```

time: 475 us -> 205 us (0.43)
  the two profiles are of different devices: /device:TPU:56 before, /device:TPU:8 now
where the time goes in v1:
time: 205 us; the launch traced here: 204 us
  waiting for transfers between devices  86.1 us (42%)
  starting transfers between devices  59.2 us (29%)
  blocking collectives  24.7 us (12%)
  local copies, waits for them, and re-layouts  12.4 us (6%)
  matrix products  11.2 us (5%)
  other arithmetic  9.26 us (5%)
    all_to_all x4, waiting for transfers between devices, scatter(): return lax.all_to_all(blocks, axis, split_axis=0, concat_axis=0, tiled=True)  49.1 us
    all_to_all x3, waiting for transfers between devices, gather(): return lax.all_to_all(wide, axis, split_axis=0, concat_axis=0, tiled=True)  33.7 us
    all_to_all x1, blocking collectives, gather(): return lax.all_to_all(wide, axis, split_axis=0, concat_axis=0, tiled=True)  24.7 us
    all_to_all x3, starting transfers between devices, gather(): return lax.all_to_all(wide, axis, split_axis=0, concat_axis=0, tiled=True)  23.5 us
    all_to_all x4, starting transfers between devices, scatter(): return lax.all_to_all(blocks, axis, split_axis=0, concat_axis=0, tiled=True)  18.2 us
    ppermute x1, starting transfers between devices, local(): term = lax.ppermute(term, ('y_lo', 'z_hi'), swap_pairs())  7.55 us
    ppermute x1, starting transfers between devices, local(): weight = lax.ppermute(out_weight.T, ('y_lo', 'z_hi'), swap_pairs())  6.11 us
    unnamed x22, local copies, waits for them, and re-layouts  4.78 us
  transfers between devices with their start and end apart: 11, of which 8 were waited for; matrix products, arithmetic and copies ran while one was open for 13% of the time, Pallas kernels for 0%

profile of v1, /device:TPU:8, one launch (start us, length us, event | category | flops | bytes accessed | tf_op | source)
XLA Modules:
  0.0 203.7 jit_solution(1478398761859786190)
XLA Ops:
  0.6 0.0 copy-start
  0.6 0.0 copy-start.8
  0.7 6.1 %collective-permute-start = (bf16[192,256]{1,0:T(8,128)(2,1)}, bf16[192,256]{1,0:T(8,128)(2,1)S(1)}, u32[]{:S(2)}, u32[]{:S(2)}) collective-permute-start(bf16[192,256]{1,0:T(8,128)(2,1)} %bitcast.109), channel_id=1, source_target_pairs={{0,0},{4,128},{8,256},{12,384},{128,4},{132,132},{136,260},{140,38... | collective-permute-start | bytes 294920 | tf_op jit(solution)/shard_map/ppermute | solution.py:43
  6.8 3.3 %collective-permute-done = bf16[192,256]{1,0:T(8,128)(2,1)S(1)} collective-permute-done((bf16[192,256]{1,0:T(8,128)(2,1)}, bf16[192,256]{1,0:T(8,128)(2,1)S(1)}, u32[]{:S(2)}, u32[]{:S(2)}) %collective-permute-start) | collective-permute-done | bytes 98336 | tf_op jit(solution)/shard_map/ppermute | solution.py:43
  10.1 0.8 broadcast_in_dim.10
  10.8 11.8 %all-to-all-start = ((bf16[4,192,256]{2,1,0:T(8,128)(2,1)}), bf16[4,192,256]{2,1,0:T(8,128)(2,1)S(1)}, u32[]{:S(2)}, u32[]{:S(2)}) async-start(bf16[4,192,256]{2,1,0:T(8,128)(2,1)} %broadcast_in_dim.10), calls=%async_computation | async-start | bytes 786432 | tf_op jit(solution)/shard_map/all_to_all | solution.py:24
  22.7 1.0 copy.102
  23.7 0.0 copy-done.8
  23.7 0.1 copy.103
  23.8 1.2 fusion.22
  25.0 0.0 copy-done
  25.0 0.5 convolution_convert_fusion
  25.5 0.0 copy-start.7
  25.5 0.1 copy.76
  25.6 4.6 %all-to-all-done = bf16[4,192,256]{2,1,0:T(8,128)(2,1)S(1)} async-done(((bf16[4,192,256]{2,1,0:T(8,128)(2,1)}), bf16[4,192,256]{2,1,0:T(8,128)(2,1)S(1)}, u32[]{:S(2)}, u32[]{:S(2)}) %all-to-all-start) | async-done | bytes 393248 | tf_op jit(solution)/shard_map/all_to_all | solution.py:24
  30.3 24.7 %all_to_all.40 = bf16[4,256,256]{2,1,0:T(8,128)(2,1)S(1)} all-to-all(bf16[4,256,256]{2,1,0:T(8,128)(2,1)S(1)} %broadcast_in_dim.13), channel_id=1, replica_groups=mesh['y_lo'=4,'x'=4,'core'=2,'z_hi'=4,'z_lo'=2,'y_hi'=2] {'z_hi'}, dimensions={0} | all-to-all | bytes 1048576 | tf_op jit(solution)/shard_map/all_to_all | solution.py:24
  55.0 1.0 broadcast_in_dim.14
  56.0 7.3 %all-to-all-start.4 = ((bf16[4,256,384]{2,1,0:T(8,128)(2,1)}), bf16[4,256,384]{2,1,0:T(8,128)(2,1)S(1)}, u32[]{:S(2)}, u32[]{:S(2)}) async-start(bf16[4,256,384]{2,1,0:T(8,128)(2,1)} %broadcast_in_dim.14), calls=%async_computation.4 | async-start | bytes 1572864 | tf_op jit(solution)/shard_map/all_to_all | solution.py:24
  63.3 22.1 %all-to-all-done.4 = bf16[4,256,384]{2,1,0:T(8,128)(2,1)S(1)} async-done(((bf16[4,256,384]{2,1,0:T(8,128)(2,1)}), bf16[4,256,384]{2,1,0:T(8,128)(2,1)S(1)}, u32[]{:S(2)}, u32[]{:S(2)}) %all-to-all-start.4) | async-done | bytes 786464 | tf_op jit(solution)/shard_map/all_to_all | solution.py:24
  85.4 1.4 broadcast_in_dim.11
  86.9 4.4 %all-to-all-start.1 = ((bf16[4,4,192,256]{3,2,1,0:T(8,128)(2,1)}), bf16[4,4,192,256]{3,2,1,0:T(8,128)(2,1)}, u32[]{:S(2)}, u32[]{:S(2)}) async-start(bf16[4,4,192,256]{3,2,1,0:T(8,128)(2,1)} %broadcast_in_dim.11), calls=%async_computation.1 | async-start | bytes 3145728 | tf_op jit(solution)/shard_map/all_to_all | solution.py:24
  91.2 2.6 %convert_bitcast_fusion = bf16[4,4,384,256]{2,3,0,1:T(8,128)(2,1)} fusion(bf16[4,256,384]{2,1,0:T(8,128)(2,1)S(1)} %all-to-all-done.4, bf16[4,256,256]{2,1,0:T(8,128)(2,1)S(1)} %all_to_all.40), kind=kOutput, calls=%fused_computation.4 | convolution fusion | flops 806879232 | bytes 4456448 | tf_op jit(solution)/shard_map/xrn,ark->xank/dot_general | solution.py:65
  93.9 3.2 %copy.86 = bf16[4,4,384,256]{3,2,1,0:T(8,128)(2,1)S(1)} copy(bf16[4,4,384,256]{2,3,0,1:T(8,128)(2,1)} %convert_bitcast_fusion) | data formatting | bytes 6291456 | tf_op jit(solution)/shard_map/convert_element_type | solution.py:65
  97.1 1.4 select_bitcast_fusion
  98.4 1.9 collective-permute-start.2
  100.3 7.0 %all-to-all-done.1 = bf16[4,4,192,256]{3,2,1,0:T(8,128)(2,1)} async-done(((bf16[4,4,192,256]{3,2,1,0:T(8,128)(2,1)}), bf16[4,4,192,256]{3,2,1,0:T(8,128)(2,1)}, u32[]{:S(2)}, u32[]{:S(2)}) %all-to-all-start.1) | async-done | bytes 1572896 | tf_op jit(solution)/shard_map/all_to_all | solution.py:24
  107.4 1.9 collective-permute-start.1
  109.3 0.0 collective-permute-done.2
  109.3 3.3 %fusion.1 = bf16[4,4,192,256]{3,2,1,0:T(8,128)(2,1)} fusion(bf16[4,4,192,256]{3,2,1,0:T(8,128)(2,1)} %collective-permute-done.2, pred[]{:T(512)S(6)} %eq.2, bf16[4,4,2,192,256]{4,3,2,1,0:T(8,128)(2,1)S(1)} %bitcast.92), kind=kLoop, calls=%fused_computation.3 | loop fusion | flops 3932160 | bytes 6291457 | tf_op jit(solution)/shard_map/convert_element_type | solution.py:69
  112.6 3.6 %all-to-all-start.6 = ((bf16[4,4,192,256]{3,2,1,0:T(8,128)(2,1)}), bf16[4,4,192,256]{3,2,1,0:T(8,128)(2,1)S(1)}, u32[]{:S(2)}, u32[]{:S(2)}) async-start(bf16[4,4,192,256]{3,2,1,0:T(8,128)(2,1)} %fusion.1), calls=%async_computation.6 | async-start | bytes 3145728 | tf_op jit(solution)/shard_map/all_to_all | solution.py:28
  116.2 0.0 collective-permute-done.1
  116.2 2.1 %select_bitcast_fusion.2 = (bf16[4,4,1,192,256]{4,3,2,1,0:T(8,128)(2,1)S(1)}, bf16[4,4,1,192,256]{4,3,2,1,0:T(8,128)(2,1)S(1)}) fusion(bf16[4,4,192,256]{3,2,1,0:T(8,128)(2,1)} %all-to-all-done.1, bf16[4,4,192,256]{3,2,1,0:T(8,128)(2,1)} %collective-permute-done.1, pred[]{:T(512)S(6)} %eq.2), kind=kLoop, calls=%fused_computation.8 | loop fusion | flops 1572864 | bytes 6291457 | tf_op jit(solution)/shard_map/stack | solution.py:49
  118.3 0.0 copy-start.4
  118.3 0.3 pad_maximum_fusion
  118.6 0.0 copy-start.5
  118.6 1.6 copy-done.5
  120.3 0.0 copy-done.4
  120.3 1.8 fusion.6
  122.1 15.7 %all-to-all-done.6 = bf16[4,4,192,256]{3,2,1,0:T(8,128)(2,1)S(1)} async-done(((bf16[4,4,192,256]{3,2,1,0:T(8,128)(2,1)}), bf16[4,4,192,256]{3,2,1,0:T(8,128)(2,1)S(1)}, u32[]{:S(2)}, u32[]{:S(2)}) %all-to-all-start.6) | async-done | bytes 1572896 | tf_op jit(solution)/shard_map/all_to_all | solution.py:28
  137.8 4.1 %all-to-all-start.5 = ((bf16[4,256,256]{1,2,0:T(8,128)(2,1)}), bf16[4,256,256]{1,2,0:T(8,128)(2,1)S(1)}, u32[]{:S(2)}, u32[]{:S(2)}) async-start(bf16[4,256,256]{1,2,0:T(8,128)(2,1)} %fusion.6), calls=%async_computation.5 | async-start | bytes 1048576 | tf_op jit(solution)/shard_map/all_to_all | solution.py:28
  141.9 1.1 reduce_sum.70
  143.0 14.3 %all-to-all-done.5 = bf16[4,256,256]{1,2,0:T(8,128)(2,1)S(1)} async-done(((bf16[4,256,256]{1,2,0:T(8,128)(2,1)}), bf16[4,256,256]{1,2,0:T(8,128)(2,1)S(1)}, u32[]{:S(2)}, u32[]{:S(2)}) %all-to-all-start.5) | async-done | bytes 524320 | tf_op jit(solution)/shard_map/all_to_all | solution.py:28
  157.3 4.8 %all-to-all-start.7 = ((bf16[4,192,256]{2,1,0:T(8,128)(2,1)}), bf16[4,192,256]{2,1,0:T(8,128)(2,1)S(1)}, u32[]{:S(2)}, u32[]{:S(2)}) async-start(bf16[4,192,256]{2,1,0:T(8,128)(2,1)} %reduce_sum.70), calls=%async_computation.7 | async-start | bytes 786432 | tf_op jit(solution)/shard_map/all_to_all | solution.py:28
  162.2 0.0 copy-done.2
  162.2 3.8 %fusion.3 = bf16[4,256,384]{1,2,0:T(8,128)(2,1)} fusion(bf16[4,4,384,256]{3,2,1,0:T(8,128)(2,1)} %bitcast.94, bf16[4,256,256]{2,1,0:T(8,128)(2,1)S(1)} %copy-done.2), kind=kOutput, calls=%fused_computation.11 | convolution fusion | flops 805699584 | bytes 4456448 | tf_op jit(solution)/shard_map/ark,xank->xrn/dot_general | solution.py:77
  166.0 0.1 reduce_sum.68
  166.1 3.5 %all-to-all-done.7 = bf16[4,192,256]{2,1,0:T(8,128)(2,1)S(1)} async-done(((bf16[4,192,256]{2,1,0:T(8,128)(2,1)}), bf16[4,192,256]{2,1,0:T(8,128)(2,1)S(1)}, u32[]{:S(2)}, u32[]{:S(2)}) %all-to-all-start.7) | async-done | bytes 393248 | tf_op jit(solution)/shard_map/all_to_all | solution.py:28
  169.6 5.7 %all-to-all-start.3 = ((bf16[4,256,384]{1,2,0:T(8,128)(2,1)}), bf16[4,256,384]{1,2,0:T(8,128)(2,1)S(1)}, u32[]{:S(2)}, u32[]{:S(2)}) async-start(bf16[4,256,384]{1,2,0:T(8,128)(2,1)} %fusion.3), calls=%async_computation.3 | async-start | bytes 1572864 | tf_op jit(solution)/shard_map/all_to_all | solution.py:28
  175.3 0.0 copy-done.6
  175.3 0.2 multiply_reduce_fusion
  175.5 0.1 multiply_convert_fusion
  175.6 0.2 fusion.8
  175.8 0.2 fusion.7
  176.0 0.1 reduce_sum.71
  176.1 7.6 %collective-permute-start.3 = (bf16[192,256]{1,0:T(8,128)(2,1)S(1)}, bf16[192,256]{1,0:T(8,128)(2,1)S(1)}, u32[]{:S(2)}, u32[]{:S(2)}) collective-permute-start(bf16[192,256]{1,0:T(8,128)(2,1)S(1)} %reduce_sum.71), channel_id=1, source_target_pairs={{0,0},{4,128},{8,256},{12,384},{128,4},{132,132},{136,260},{140,38... | collective-permute-start | bytes 294920 | tf_op jit(solution)/shard_map/ppermute | solution.py:72
  183.7 0.6 convolution_convert_fusion.1
  184.2 0.8 copy.88
  185.0 0.8 copy.89
  185.8 0.8 copy.90
  186.5 15.5 %all-to-all-done.3 = bf16[4,256,384]{1,2,0:T(8,128)(2,1)S(1)} async-done(((bf16[4,256,384]{1,2,0:T(8,128)(2,1)}), bf16[4,256,384]{1,2,0:T(8,128)(2,1)S(1)}, u32[]{:S(2)}, u32[]{:S(2)}) %all-to-all-start.3) | async-done | bytes 786464 | tf_op jit(solution)/shard_map/all_to_all | solution.py:28
  202.1 0.2 reduce_sum.67
  202.2 0.8 copy.87
  203.0 0.0 collective-permute-done.3
  203.0 0.7 convert_bitcast_fusion.1
  (8 shorter events, 0.0 us)
Async XLA Ops:
  0.6 24.3 %copy-start = (bf16[256,256]{1,0:T(8,128)(2,1)S(1)}, bf16[256,256]{1,0:T(8,128)(2,1)}, u32[]{:S(2)}) copy-start(bf16[256,256]{1,0:T(8,128)(2,1)} %param.7) | copy-start | bytes 393220
  0.6 23.0 %copy-start.8 = (bf16[256,256]{1,0:T(8,128)(2,1)S(1)}, bf16[256,256]{1,0:T(8,128)(2,1)}, u32[]{:S(2)}) copy-start(bf16[256,256]{1,0:T(8,128)(2,1)} %param.6) | copy-start | bytes 393220
  0.7 9.4 %collective-permute-start = (bf16[192,256]{1,0:T(8,128)(2,1)}, bf16[192,256]{1,0:T(8,128)(2,1)S(1)}, u32[]{:S(2)}, u32[]{:S(2)}) collective-permute-start(bf16[192,256]{1,0:T(8,128)(2,1)} %bitcast.109), channel_id=1, source_target_pairs={{0,0},{4,128},{8,256},{12,384},{128,4},{132,132},{136,260},{140,38... | collective-permute-start | bytes 294920 | tf_op jit(solution)/shard_map/ppermute | solution.py:43
  10.8 19.4 %all-to-all-start = ((bf16[4,192,256]{2,1,0:T(8,128)(2,1)}), bf16[4,192,256]{2,1,0:T(8,128)(2,1)S(1)}, u32[]{:S(2)}, u32[]{:S(2)}) async-start(bf16[4,192,256]{2,1,0:T(8,128)(2,1)} %broadcast_in_dim.10), calls=%async_computation | async-start | bytes 786432 | tf_op jit(solution)/shard_map/all_to_all | solution.py:24
  25.5 29.5 %copy-start.7 = (bf16[256,384]{1,0:T(8,128)(2,1)S(1)}, bf16[256,384]{1,0:T(8,128)(2,1)}, u32[]{:S(2)}) copy-start(bf16[256,384]{1,0:T(8,128)(2,1)} %param.9) | copy-start | bytes 589828
  55.0 36.2 %copy-start.1 = (bf16[4,256,256]{2,1,0:T(8,128)(2,1)}, bf16[4,256,256]{2,1,0:T(8,128)(2,1)S(1)}, u32[]{:S(2)}) copy-start(bf16[4,256,256]{2,1,0:T(8,128)(2,1)S(1)} %all_to_all.40) | copy-start | bytes 1572868
  56.0 29.4 %all-to-all-start.4 = ((bf16[4,256,384]{2,1,0:T(8,128)(2,1)}), bf16[4,256,384]{2,1,0:T(8,128)(2,1)S(1)}, u32[]{:S(2)}, u32[]{:S(2)}) async-start(bf16[4,256,384]{2,1,0:T(8,128)(2,1)} %broadcast_in_dim.14), calls=%async_computation.4 | async-start | bytes 1572864 | tf_op jit(solution)/shard_map/all_to_all | solution.py:24
  85.4 5.8 %copy-start.3 = (bf16[4,256,384]{2,1,0:T(8,128)(2,1)}, bf16[4,256,384]{2,1,0:T(8,128)(2,1)S(1)}, u32[]{:S(2)}) copy-start(bf16[4,256,384]{2,1,0:T(8,128)(2,1)S(1)} %all-to-all-done.4) | copy-start | bytes 2359300
  86.9 20.5 %all-to-all-start.1 = ((bf16[4,4,192,256]{3,2,1,0:T(8,128)(2,1)}), bf16[4,4,192,256]{3,2,1,0:T(8,128)(2,1)}, u32[]{:S(2)}, u32[]{:S(2)}) async-start(bf16[4,4,192,256]{3,2,1,0:T(8,128)(2,1)} %broadcast_in_dim.11), calls=%async_computation.1 | async-start | bytes 3145728 | tf_op jit(solution)/shard_map/all_to_all | solution.py:24
  98.4 10.9 %collective-permute-start.2 = (bf16[4,4,192,256]{3,2,1,0:T(8,128)(2,1)}, bf16[4,4,192,256]{3,2,1,0:T(8,128)(2,1)}, u32[]{:S(2)}, u32[]{:S(2)}) collective-permute-start(bf16[4,4,192,256]{3,2,1,0:T(8,128)(2,1)} %select_bitcast_fusion), channel_id=1, source_target_pairs={{0,16},{16,0},{1,17},{17,1},{2,18},{18,2},{3,19},{19,3},{4,20},{20... | collective-permute-start | bytes 4718600 | tf_op jit(solution)/shard_map/ppermute | solution.py:36
  107.4 8.8 %collective-permute-start.1 = (bf16[4,4,192,256]{3,2,1,0:T(8,128)(2,1)}, bf16[4,4,192,256]{3,2,1,0:T(8,128)(2,1)}, u32[]{:S(2)}, u32[]{:S(2)}) collective-permute-start(bf16[4,4,192,256]{3,2,1,0:T(8,128)(2,1)} %all-to-all-done.1), channel_id=1, source_target_pairs={{0,16},{16,0},{1,17},{17,1},{2,18},{18,2},{3,19},{19,3},{4,20},{20... | collective-permute-start | bytes 4718600 | tf_op jit(solution)/shard_map/ppermute | solution.py:36
  112.6 25.2 %all-to-all-start.6 = ((bf16[4,4,192,256]{3,2,1,0:T(8,128)(2,1)}), bf16[4,4,192,256]{3,2,1,0:T(8,128)(2,1)S(1)}, u32[]{:S(2)}, u32[]{:S(2)}) async-start(bf16[4,4,192,256]{3,2,1,0:T(8,128)(2,1)} %fusion.1), calls=%async_computation.6 | async-start | bytes 3145728 | tf_op jit(solution)/shard_map/all_to_all | solution.py:28
  118.3 2.0 copy-start.4
  118.6 1.7 copy-start.5
  137.8 19.5 %all-to-all-start.5 = ((bf16[4,256,256]{1,2,0:T(8,128)(2,1)}), bf16[4,256,256]{1,2,0:T(8,128)(2,1)S(1)}, u32[]{:S(2)}, u32[]{:S(2)}) async-start(bf16[4,256,256]{1,2,0:T(8,128)(2,1)} %fusion.6), calls=%async_computation.5 | async-start | bytes 1048576 | tf_op jit(solution)/shard_map/all_to_all | solution.py:28
  141.9 20.2 %copy-start.2 = (bf16[4,256,256]{2,1,0:T(8,128)(2,1)S(1)}, bf16[4,256,256]{2,1,0:T(8,128)(2,1)}, u32[]{:S(2)}) copy-start(bf16[4,256,256]{2,1,0:T(8,128)(2,1)} %copy-done.1) | copy-start | bytes 1572868
  157.3 12.2 %all-to-all-start.7 = ((bf16[4,192,256]{2,1,0:T(8,128)(2,1)}), bf16[4,192,256]{2,1,0:T(8,128)(2,1)S(1)}, u32[]{:S(2)}, u32[]{:S(2)}) async-start(bf16[4,192,256]{2,1,0:T(8,128)(2,1)} %reduce_sum.70), calls=%async_computation.7 | async-start | bytes 786432 | tf_op jit(solution)/shard_map/all_to_all | solution.py:28
  166.0 9.3 %copy-start.6 = (f32[2,256,256]{1,2,0:T(8,128)S(1)}, f32[2,256,256]{1,2,0:T(8,128)}, u32[]{:S(2)}) copy-start(f32[2,256,256]{1,2,0:T(8,128)} %get-tuple-element.28) | copy-start | bytes 1572868
  169.6 32.5 %all-to-all-start.3 = ((bf16[4,256,384]{1,2,0:T(8,128)(2,1)}), bf16[4,256,384]{1,2,0:T(8,128)(2,1)S(1)}, u32[]{:S(2)}, u32[]{:S(2)}) async-start(bf16[4,256,384]{1,2,0:T(8,128)(2,1)} %fusion.3), calls=%async_computation.3 | async-start | bytes 1572864 | tf_op jit(solution)/shard_map/all_to_all | solution.py:28
  176.1 26.9 %collective-permute-start.3 = (bf16[192,256]{1,0:T(8,128)(2,1)S(1)}, bf16[192,256]{1,0:T(8,128)(2,1)S(1)}, u32[]{:S(2)}, u32[]{:S(2)}) collective-permute-start(bf16[192,256]{1,0:T(8,128)(2,1)S(1)} %reduce_sum.71), channel_id=1, source_target_pairs={{0,0},{4,128},{8,256},{12,384},{128,4},{132,132},{136,260},{140,38... | collective-permute-start | bytes 294920 | tf_op jit(solution)/shard_map/ppermute | solution.py:72

commit v2 on v1

v2 whole, which is shorter than its diff:
```python
import math

import jax
import jax.numpy as jnp
from jax import lax
from jax.experimental import pallas as pl
from jax.experimental.pallas import tpu as pltpu
from jax.sharding import Mesh, PartitionSpec as P

HEAD = 128
PATCHES = 256
FACTOR = 1.0 / math.sqrt(HEAD)
AXES = ("y_lo", "x", "core", "z", "y_hi")
SIZES = (4, 4, 2, 8, 2)
ROWS = ("y_lo", "x", "core")
COLS = ("z", "y_hi")
BF16 = jnp.bfloat16
F32 = jnp.float32
STRIP = 192
TN = (((0,), (0,)), ((), ()))
NT = (((1,), (1,)), ((), ()))
NN = (((1,), (0,)), ((), ()))


def dot(a, b, dims):
    return lax.dot_general(a, b, dims, preferred_element_type=F32)


def call(body, outs, scratch, flops, size, n_in, scalars=False, vmem_mib=40):
    vmem = pl.BlockSpec(memory_space=pltpu.VMEM)
    smem = pl.BlockSpec(memory_space=pltpu.SMEM)
    return pl.pallas_call(
        body,
        out_shape=[jax.ShapeDtypeStruct(s, t) for s, t in outs],
        in_specs=([smem] if scalars else []) + [vmem] * n_in,
        out_specs=[vmem] * len(outs),
        scratch_shapes=scratch,
        compiler_params=pltpu.CompilerParams(vmem_limit_bytes=vmem_mib * 2**20),
        cost_estimate=pl.CostEstimate(flops=flops, bytes_accessed=size, transcendentals=0),
    )


def attend(q_ref, k_ref, v_ref, ctx_ref, probs_ref):
    for h in range(2):
        cols = slice(h * HEAD, (h + 1) * HEAD)
        scores = dot(q_ref[:, cols], k_ref[:, cols], NT) * FACTOR
        exponent = jnp.exp(scores - jnp.max(scores, axis=-1, keepdims=True))
        probs = exponent / jnp.sum(exponent, axis=-1, keepdims=True)
        probs_ref[h] = probs
        ctx_ref[:, cols] = dot(probs.astype(BF16), v_ref[:, cols], NN).astype(BF16)


def attend_back(q_ref, k_ref, v_ref, probs_ref, dctx_ref, gq_ref, gk_ref, gv_ref):
    for h in range(2):
        cols = slice(h * HEAD, (h + 1) * HEAD)
        dctx = dctx_ref[:, cols]
        probs = probs_ref[h]
        gv_ref[:, cols] = dot(probs.astype(BF16), dctx, TN).astype(BF16)
        dprobs = dot(dctx, v_ref[:, cols], NT)
        center = jnp.sum(probs * dprobs, axis=-1, keepdims=True)
        dscores = (probs * (dprobs - center)).astype(BF16)
        gq_ref[:, cols] = (dot(dscores, k_ref[:, cols], NN) * FACTOR).astype(BF16)
        gk_ref[:, cols] = (dot(dscores, q_ref[:, cols], TN) * FACTOR).astype(BF16)


def turn_cot(where_ref, own_ref, far_ref, mine_ref, theirs_ref, work):
    core = where_ref[0]
    for slot, cot in enumerate((own_ref, far_ref)):
        work[...] = cot[...].astype(F32).T.astype(BF16)
        rows = slice(slot * STRIP, (slot + 1) * STRIP)
        mine_ref[rows, :] = work[pl.ds(pl.multiple_of(core * STRIP, 16), STRIP), :]
        theirs_ref[rows, :] = work[pl.ds(pl.multiple_of((1 - core) * STRIP, 16), STRIP), :]


def weight_term(where_ref, ctx_ref, other_ctx_ref, cot_ref, other_cot_ref, term_ref):
    half = where_ref[1]
    for z in range(8):
        term = dot(cot_ref[...], ctx_ref[z], NN) + dot(other_cot_ref[...], other_ctx_ref[z], NN)
        for slot in range(2):
            x = 2 * (z % 2) + (half if slot == 0 else 1 - half)
            term_ref[x, z // 2] = term[slot * STRIP : (slot + 1) * STRIP].astype(BF16)


def add_up(blocks_ref, sum_ref):
    for y in range(4):
        sum_ref[y] = sum(blocks_ref[x, y].astype(F32) for x in range(4)).astype(BF16)


def project(
    where_ref, ctx_ref, own_ref, far_ref, near_w_ref, far_w_ref,
    dctx_ref, keep_ref, send_ref, weight, ctx
):
    core, half = where_ref[0], where_ref[1]
    near_row = pl.multiple_of(core * STRIP, 16)
    far_row = pl.multiple_of((1 - core) * STRIP, 16)
    for z in range(8):
        cols = slice(z * 256, (z + 1) * 256)
        ctx[:, cols] = ctx_ref[z]
        for slot in range(2):
            x = 2 * (z % 2) + (half if slot == 0 else 1 - half)
            weight[slot, pl.ds(near_row, STRIP), cols] = near_w_ref[x, z // 2]
            weight[slot, pl.ds(far_row, STRIP), cols] = far_w_ref[x, z // 2]
    for z in range(8):
        cols = slice(z * 256, (z + 1) * 256)
        part = dot(own_ref[...], weight[0, :, cols], NN) + dot(far_ref[...], weight[1, :, cols], NN)
        dctx_ref[z] = part.astype(BF16)
    keep_ref[...] = dot(ctx[...], weight[0], NT).astype(BF16)
    send_ref[...] = dot(ctx[...], weight[1], NT).astype(BF16)


def plane_pairs():
    pairs = []
    for y in range(4):
        for x in range(4):
            for z in range(8):
                there = (z // 2, 2 * (z % 2) + x % 2, 2 * y + x // 2)
                pairs.append(((y * 4 + x) * 8 + z, (there[0] * 4 + there[1]) * 8 + there[2]))
    return pairs


def change_plane(block):
    return lax.ppermute(block, ("y_lo", "x", "z"), plane_pairs())


def gather(block, axis, count):
    wide = jnp.broadcast_to(block[None], (count,) + block.shape)
    return lax.all_to_all(wide, axis, split_axis=0, concat_axis=0, tiled=True)


def scatter(blocks, axis):
    return lax.all_to_all(blocks, axis, split_axis=0, concat_axis=0, tiled=True)


def total(blocks):
    return sum(b.astype(F32) for b in blocks)


def swap(block, axis):
    return lax.ppermute(block, axis, [(0, 1), (1, 0)])


def local(query_rows, key_rows, value_rows, out_weight, grad_out):
    core, half = lax.axis_index("core"), lax.axis_index("y_hi")
    where = jnp.stack([core, half]).astype(jnp.int32)
    square = ((256, 256), BF16)
    wide = ((256, 384), BF16)

    context, probs = call(
        attend, [square, ((2, 256, 256), F32)], [], 2**26, 2**20, 3, vmem_mib=60
    )(query_rows, key_rows, value_rows)
    ctx = lax.all_gather(context, "z", axis=0)

    weight = change_plane(out_weight.T)
    grad_out, context = lax.optimization_barrier((grad_out, context))
    far_cot = swap(grad_out, "y_hi")
    weight = lax.all_gather(weight, "y_lo", axis=0)
    weight, far_cot = lax.optimization_barrier((weight, far_cot))
    near = gather(weight, "x", 4)

    strips = ((2 * STRIP, 256), BF16)
    cot_mine, cot_theirs = call(
        turn_cot, [strips, strips], [pltpu.VMEM((384, 256), BF16)], 2**20, 2**20, 2, True, vmem_mib=4
    )(where, grad_out, far_cot)
    other_cot = swap(cot_theirs, "core")
    other_ctx = swap(ctx, "core")
    term = call(
        weight_term, [((4, 4, STRIP, 256), BF16)], [], 2**29, 2**22, 4, True, vmem_mib=60
    )(where, ctx, other_ctx, cot_mine, other_cot)[0]
    near, term = lax.optimization_barrier((near, term))
    far = swap(near, "core")
    term = scatter(term, "x")
    term = call(add_up, [((4, STRIP, 256), BF16)], [], 2**20, 2**21, 1, vmem_mib=4)(term)[0]

    dctx, keep, send = call(
        project,
        [((8, 256, 256), BF16), wide, wide],
        [pltpu.VMEM((2, 384, 2048), BF16), pltpu.VMEM((256, 2048), BF16)],
        2**30,
        2**23,
        5,
        True,
        vmem_mib=60,
    )(where, ctx, grad_out, far_cot, near, far)
    dctx = lax.psum_scatter(dctx, "z", scatter_dimension=0, tiled=True)[0]
    received = swap(send, "y_hi")
    layer_out = total([keep, received]).astype(BF16)
    term, received = lax.optimization_barrier((term, received))
    term = total(scatter(term, "y_lo")).astype(BF16)
    grad_weight = change_plane(term).T.astype(F32)
    grad_query, grad_key, grad_value = call(
        attend_back, [square] * 3, [], 2**27, 2**21, 5, vmem_mib=60
    )(query_rows, key_rows, value_rows, probs, dctx)
    return (layer_out, grad_query, grad_key, grad_value, grad_weight)


def solution(mesh):
    fine = Mesh(mesh.devices.reshape(SIZES), AXES)
    rows_cols, cols_rows = P(ROWS, COLS), P(COLS, ROWS)
    in_specs = (rows_cols, rows_cols, rows_cols, cols_rows, rows_cols)
    out_specs = (rows_cols, rows_cols, rows_cols, rows_cols, cols_rows)
    return jax.shard_map(local, mesh=fine, in_specs=in_specs, out_specs=out_specs, check_vma=False)
```

time: 205 us -> 149 us (0.73)
  the two profiles are of different devices: /device:TPU:8 before, /device:TPU:58 now
where the time goes in v2:
time: 149 us
  starting transfers between devices  45.1 us (30%)
  waiting for transfers between devices  35.4 us (24%)
  blocking collectives  33.2 us (22%)
  Pallas kernels  16.1 us (11%)
  between operations  14.2 us (10%)
  local copies, waits for them, and re-layouts  3.02 us (2%)
  other arithmetic  1.55 us (1%)
    ppermute x2, starting transfers between devices, change_plane(): return lax.ppermute(block, ('y_lo', 'x', 'z'), plane_pairs())  21.1 us
    all_gather x1, blocking collectives, local(): weight = lax.all_gather(weight, 'y_lo', axis=0)  18.9 us
    all_to_all x1, blocking collectives, scatter(): return lax.all_to_all(blocks, axis, split_axis=0, concat_axis=0, tiled=True)  14.4 us
    ppermute x5, starting transfers between devices, swap(): return lax.ppermute(block, axis, [(0, 1), (1, 0)])  12.2 us
    all_to_all x1, waiting for transfers between devices, scatter(): return lax.all_to_all(blocks, axis, split_axis=0, concat_axis=0, tiled=True)  10.4 us
    ppermute x2, waiting for transfers between devices, change_plane(): return lax.ppermute(block, ('y_lo', 'x', 'z'), plane_pairs())  9.94 us
    reduce_scatter x1, waiting for transfers between devices, local(): dctx = lax.psum_scatter(dctx, 'z', scatter_dimension=0, tiled=True)[0]  9.93 us
    all_to_all x1, starting transfers between devices, gather(): return lax.all_to_all(wide, axis, split_axis=0, concat_axis=0, tiled=True)  6.77 us
  transfers between devices with their start and end apart: 11, of which 8 were waited for; matrix products, arithmetic and copies ran while one was open for 2% of the time, Pallas kernels for 7%

profile of v2, /device:TPU:58, one launch (start us, length us, event | category | flops | bytes accessed | tf_op | source)
XLA Modules:
  0.0 148.5 jit_solution(7314550008008692741)
XLA Ops:
  7.2 0.0 all-gather.4.cloned.1.call-start
  7.2 2.7 %shard_map.92 = (bf16[256,256]{1,0:T(8,128)(2,1)}, f32[2,256,256]{2,1,0:T(8,128)}) custom-call(bf16[256,256]{1,0:T(8,128)(2,1)} %q_ref.3, bf16[256,256]{1,0:T(8,128)(2,1)} %k_ref.3, bf16[256,256]{1,0:T(8,128)(2,1)} %v_ref.3), custom_call_target="tpu_custom_call" | custom-call | flops 67108864 | bytes 1048576 | tf_op jit(solution)/shard_map/pallas_call | solution.py:148
  9.9 0.0 all-gather.4.cloned.1.call-update
  9.9 13.3 %collective-permute-start = (bf16[192,256]{1,0:T(8,128)(2,1)}, bf16[192,256]{1,0:T(8,128)(2,1)S(1)}, u32[]{:S(2)}, u32[]{:S(2)}) collective-permute-start(bf16[192,256]{1,0:T(8,128)(2,1)} %bitcast.15), channel_id=1, source_target_pairs={{0,0},{2,64},{4,128},{6,192},{8,256},{10,320},{12,384},{14,448},{3... | collective-permute-start | bytes 294920 | tf_op jit(solution)/shard_map/ppermute | solution.py:122
  23.2 2.0 %collective-permute-start.1 = (bf16[256,384]{1,0:T(8,128)(2,1)}, bf16[256,384]{1,0:T(8,128)(2,1)S(1)}, u32[]{:S(2)}, u32[]{:S(2)}) collective-permute-start(bf16[256,384]{1,0:T(8,128)(2,1)} %own_ref.1), channel_id=1, source_target_pairs={{0,1},{1,0},{2,3},{3,2},{4,5},{5,4},{6,7},{7,6},{8,9},{9,8},{10,11... | collective-permute-start | bytes 589832 | tf_op jit(solution)/shard_map/ppermute | solution.py:139
  25.2 5.0 %collective-permute-done = bf16[192,256]{1,0:T(8,128)(2,1)S(1)} collective-permute-done((bf16[192,256]{1,0:T(8,128)(2,1)}, bf16[192,256]{1,0:T(8,128)(2,1)S(1)}, u32[]{:S(2)}, u32[]{:S(2)}) %collective-permute-start) | collective-permute-done | bytes 98336 | tf_op jit(solution)/shard_map/ppermute | solution.py:122
  30.2 18.9 %all-gather.1 = bf16[768,256]{1,0:T(8,128)(2,1)S(1)} all-gather(bf16[192,256]{1,0:T(8,128)(2,1)S(1)} %collective-permute-done), channel_id=3, replica_groups=mesh['y_lo'=4,'x'=4,'core'=2,'z'=8,'y_hi'=2] {'y_lo'}, dimensions={0}, use_global_device_ids=true | all-gather | bytes 491520 | tf_op jit(solution)/shard_map/all_gather | solution.py:156
  49.1 0.0 collective-permute-done.1.far_ref
  49.1 0.0 copy-start.1
  49.1 1.3 broadcast_in_dim.2
  50.4 0.0 copy-start
  50.4 6.8 %all-to-all-start = ((bf16[4,4,192,256]{3,2,1,0:T(8,128)(2,1)}), bf16[4,4,192,256]{3,2,1,0:T(8,128)(2,1)S(1)}, u32[]{:S(2)}, u32[]{:S(2)}) async-start(bf16[4,4,192,256]{3,2,1,0:T(8,128)(2,1)} %broadcast_in_dim.2), calls=%async_computation | async-start | bytes 3145728 | tf_op jit(solution)/shard_map/all_to_all | solution.py:127
  57.2 1.0 all-gather.4.cloned.1.call-done
  58.2 1.9 %collective-permute-start.2 = (bf16[8,256,256]{2,1,0:T(8,128)(2,1)}, bf16[8,256,256]{2,1,0:T(8,128)(2,1)S(1)}, u32[]{:S(2)}, u32[]{:S(2)}) collective-permute-start(bf16[8,256,256]{2,1,0:T(8,128)(2,1)} %bitcast.10), channel_id=1, source_target_pairs={{0,16},{16,0},{1,17},{17,1},{2,18},{18,2},{3,19},{19,3},{4,20},{20... | collective-permute-start | bytes 3145736 | tf_op jit(solution)/shard_map/ppermute | solution.py:139
  60.1 0.1 pad_add_fusion.where_ref
  60.2 0.0 copy-done.1
  60.2 0.0 copy-done
  60.2 0.0 copy-start.3
  60.2 0.7 shard_map.93
  61.0 0.0 copy-start.2
  61.0 0.7 copy-done.2
  61.6 2.4 %collective-permute-start.3 = (bf16[384,256]{1,0:T(8,128)(2,1)S(1)}, bf16[384,256]{1,0:T(8,128)(2,1)S(1)}, u32[]{:S(2)}, u32[]{:S(2)}) collective-permute-start(bf16[384,256]{1,0:T(8,128)(2,1)S(1)} %get-tuple-element.26), channel_id=1, source_target_pairs={{0,16},{16,0},{1,17},{17,1},{2,18},{18,2},{3,19},{19,3},{4,20},{20... | collective-permute-start | bytes 589832 | tf_op jit(solution)/shard_map/ppermute | solution.py:139
  64.0 1.0 collective-permute-done.3.other_cot_ref
  65.1 0.0 copy-start.6
  65.1 0.0 collective-permute-done.2.other_ctx_ref
  65.1 0.0 copy-start.5
  65.1 0.0 copy-done.3
  65.1 0.7 copy-done.6
  65.8 0.4 copy-done.5
  66.1 3.9 %shard_map.94 = bf16[4,4,192,256]{3,2,1,0:T(8,128)(2,1)} custom-call(s32[2]{0:T(128)} %copy-done.3, bf16[8,256,256]{2,1,0:T(8,128)(2,1)} %bitcast.11, bf16[8,256,256]{2,1,0:T(8,128)(2,1)} %copy-done.5, bf16[384,256]{1,0:T(8,128)(2,1)} %copy-done.2, bf16[384,256]{1,0:T(8,128)(2,1)} %copy-done.6), custom_call_target="tpu_custom_call" | custom-call | flops 536870912 | bytes 4194304 | tf_op jit(solution)/shard_map/pallas_call | solution.py:166
  70.0 0.6 all-to-all-done.near_w_ref
  70.6 0.0 copy-start.4
  70.6 1.9 %collective-permute-start.4 = (bf16[4,4,192,256]{3,2,1,0:T(8,128)(2,1)S(1)}, bf16[4,4,192,256]{3,2,1,0:T(8,128)(2,1)}, u32[]{:S(2)}, u32[]{:S(2)}) collective-permute-start(bf16[4,4,192,256]{3,2,1,0:T(8,128)(2,1)S(1)} %all-to-all-done.near_w_ref), channel_id=1, source_target_pairs={{0,16},{16,0},{1,17},{17,1},{2,18},{18,2},{3,19},{19,3},{4,20},{20... | collective-permute-start | bytes 4718600 | tf_op jit(solution)/shard_map/ppermute | solution.py:139
  72.5 0.0 copy-done.4
  72.5 5.0 %all-to-all-start.1 = ((bf16[4,4,192,256]{3,2,1,0:T(8,128)(2,1)}), bf16[4,4,192,256]{3,2,1,0:T(8,128)(2,1)S(1)}, u32[]{:S(2)}, u32[]{:S(2)}) async-start(bf16[4,4,192,256]{3,2,1,0:T(8,128)(2,1)} %shard_map.94), calls=%async_computation.2 | async-start | bytes 3145728 | tf_op jit(solution)/shard_map/all_to_all | solution.py:131
  77.5 0.0 reduce-scatter.2.cloned.1.call-start
  77.5 0.0 collective-permute-done.4.far_w_ref
  77.5 5.8 %shard_map.95 = (bf16[8,256,256]{2,1,0:T(8,128)(2,1)}, bf16[256,384]{1,0:T(8,128)(2,1)}, bf16[256,384]{1,0:T(8,128)(2,1)}) custom-call(s32[2]{0:T(128)} %copy-done.3, bf16[8,256,256]{2,1,0:T(8,128)(2,1)} %bitcast.12, bf16[256,384]{1,0:T(8,128)(2,1)} %own_ref.1, bf16[256,384]{1,0:T(8,128)(2,1)} %copy-done.1, bf16[4,4,192,256]{3,2,1,0:T(8,128)(2,1)} %copy-done.4, ...), custom_call_target="tpu_custom_call" | custom-call | flops 1073741824 | bytes 8388608 | tf_op jit(solution)/shard_map/pallas_call | solution.py:174
  83.4 0.0 reduce-scatter.2.cloned.1.call-update
  83.4 0.0 copy-start.7
  83.4 3.9 %collective-permute-start.5 = (bf16[256,384]{1,0:T(8,128)(2,1)}, bf16[256,384]{1,0:T(8,128)(2,1)S(1)}, u32[]{:S(2)}, u32[]{:S(2)}) collective-permute-start(bf16[256,384]{1,0:T(8,128)(2,1)} %get-tuple-element.29), channel_id=1, source_target_pairs={{0,1},{1,0},{2,3},{3,2},{4,5},{5,4},{6,7},{7,6},{8,9},{9,8},{10,11... | collective-permute-start | bytes 589832 | tf_op jit(solution)/shard_map/ppermute | solution.py:139
  87.3 10.4 %all-to-all-done.1.blocks_ref = bf16[4,4,192,256]{3,2,1,0:T(8,128)(2,1)S(1)} async-done(((bf16[4,4,192,256]{3,2,1,0:T(8,128)(2,1)}), bf16[4,4,192,256]{3,2,1,0:T(8,128)(2,1)S(1)}, u32[]{:S(2)}, u32[]{:S(2)}) %all-to-all-start.1) | async-done | bytes 1572896 | tf_op jit(solution)/shard_map/all_to_all | solution.py:131
  97.7 0.2 shard_map.97
  97.9 2.4 %collective-permute-done.5 = bf16[256,384]{1,0:T(8,128)(2,1)S(1)} collective-permute-done((bf16[256,384]{1,0:T(8,128)(2,1)}, bf16[256,384]{1,0:T(8,128)(2,1)S(1)}, u32[]{:S(2)}, u32[]{:S(2)}) %collective-permute-start.5) | collective-permute-done | bytes 196640 | tf_op jit(solution)/shard_map/ppermute | solution.py:139
  100.3 14.4 %all_to_all.15 = bf16[4,192,256]{2,1,0:T(8,128)(2,1)S(1)} all-to-all(bf16[4,192,256]{2,1,0:T(8,128)(2,1)S(1)} %shard_map.97), channel_id=1, replica_groups=mesh['y_lo'=4,'x'=4,'core'=2,'z'=8,'y_hi'=2] {'y_lo'}, dimensions={0} | all-to-all | bytes 786432 | tf_op jit(solution)/shard_map/all_to_all | solution.py:131
  114.7 0.1 fusion
  114.7 7.8 %collective-permute-start.6 = (bf16[192,256]{1,0:T(8,128)(2,1)S(1)}, bf16[192,256]{1,0:T(8,128)(2,1)S(1)}, u32[]{:S(2)}, u32[]{:S(2)}) collective-permute-start(bf16[192,256]{1,0:T(8,128)(2,1)S(1)} %fusion), channel_id=1, source_target_pairs={{0,0},{2,64},{4,128},{6,192},{8,256},{10,320},{12,384},{14,448},{3... | collective-permute-start | bytes 294920 | tf_op jit(solution)/shard_map/ppermute | solution.py:122
  122.6 0.0 copy-done.7
  122.6 0.7 add_convert_fusion
  123.3 4.9 %collective-permute-done.6 = bf16[192,256]{1,0:T(8,128)(2,1)S(1)} collective-permute-done((bf16[192,256]{1,0:T(8,128)(2,1)S(1)}, bf16[192,256]{1,0:T(8,128)(2,1)S(1)}, u32[]{:S(2)}, u32[]{:S(2)}) %collective-permute-start.6) | collective-permute-done | bytes 98336 | tf_op jit(solution)/shard_map/ppermute | solution.py:122
  128.2 0.7 convert_bitcast_fusion
  128.9 9.9 %reduce-scatter.2.cloned.1.call-done = bf16[1,256,256]{2,1,0:T(8,128)(2,1)} async-done(((bf16[8,256,256]{2,1,0:T(8,128)(2,1)}), bf16[1,256,256]{2,1,0:T(8,128)(2,1)}) %reduce-scatter.2.cloned.1.call-update) | async-done | bytes 131088 | tf_op jit(solution)/shard_map/reduce_scatter | solution.py:184
  138.9 2.8 %shard_map.96 = (bf16[256,256]{1,0:T(8,128)(2,1)}, bf16[256,256]{1,0:T(8,128)(2,1)}, bf16[256,256]{1,0:T(8,128)(2,1)}) custom-call(bf16[256,256]{1,0:T(8,128)(2,1)} %q_ref.3, bf16[256,256]{1,0:T(8,128)(2,1)} %k_ref.3, bf16[256,256]{1,0:T(8,128)(2,1)} %v_ref.3, f32[2,256,256]{2,1,0:T(8,128)} %get-tuple-element.30.probs_ref, bf16[256,256]{1,0:T(8,128)(2,1)} %bitcast.14), custom_call_target="tpu_custom_call" | custom-call | flops 134217728 | bytes 2097152 | tf_op jit(solution)/shard_map/pallas_call | solution.py:190
Async XLA Ops:
  7.2 51.1 %all-gather.4.cloned.1.call-start = ((), (), s32[]{:S(2)}) async-start(), calls=%async_computation.5 | async-start | bytes 1179648 | tf_op jit(solution)/shard_map/all_gather | solution.py:151
  9.9 20.3 %collective-permute-start = (bf16[192,256]{1,0:T(8,128)(2,1)}, bf16[192,256]{1,0:T(8,128)(2,1)S(1)}, u32[]{:S(2)}, u32[]{:S(2)}) collective-permute-start(bf16[192,256]{1,0:T(8,128)(2,1)} %bitcast.15), channel_id=1, source_target_pairs={{0,0},{2,64},{4,128},{6,192},{8,256},{10,320},{12,384},{14,448},{3... | collective-permute-start | bytes 294920 | tf_op jit(solution)/shard_map/ppermute | solution.py:122
  23.2 25.9 %collective-permute-start.1 = (bf16[256,384]{1,0:T(8,128)(2,1)}, bf16[256,384]{1,0:T(8,128)(2,1)S(1)}, u32[]{:S(2)}, u32[]{:S(2)}) collective-permute-start(bf16[256,384]{1,0:T(8,128)(2,1)} %own_ref.1), channel_id=1, source_target_pairs={{0,1},{1,0},{2,3},{3,2},{4,5},{5,4},{6,7},{7,6},{8,9},{9,8},{10,11... | collective-permute-start | bytes 589832 | tf_op jit(solution)/shard_map/ppermute | solution.py:139
  49.1 11.1 %copy-start.1 = (bf16[256,384]{1,0:T(8,128)(2,1)}, bf16[256,384]{1,0:T(8,128)(2,1)S(1)}, u32[]{:S(2)}) copy-start(bf16[256,384]{1,0:T(8,128)(2,1)S(1)} %collective-permute-done.1.far_ref) | copy-start | bytes 589828
  50.4 9.8 %copy-start = (bf16[256,384]{1,0:T(8,128)(2,1)S(1)}, bf16[256,384]{1,0:T(8,128)(2,1)}, u32[]{:S(2)}) copy-start(bf16[256,384]{1,0:T(8,128)(2,1)} %own_ref.1) | copy-start | bytes 589828
  50.4 20.2 %all-to-all-start = ((bf16[4,4,192,256]{3,2,1,0:T(8,128)(2,1)}), bf16[4,4,192,256]{3,2,1,0:T(8,128)(2,1)S(1)}, u32[]{:S(2)}, u32[]{:S(2)}) async-start(bf16[4,4,192,256]{3,2,1,0:T(8,128)(2,1)} %broadcast_in_dim.2), calls=%async_computation | async-start | bytes 3145728 | tf_op jit(solution)/shard_map/all_to_all | solution.py:127
  58.2 6.9 %collective-permute-start.2 = (bf16[8,256,256]{2,1,0:T(8,128)(2,1)}, bf16[8,256,256]{2,1,0:T(8,128)(2,1)S(1)}, u32[]{:S(2)}, u32[]{:S(2)}) collective-permute-start(bf16[8,256,256]{2,1,0:T(8,128)(2,1)} %bitcast.10), channel_id=1, source_target_pairs={{0,16},{16,0},{1,17},{17,1},{2,18},{18,2},{3,19},{19,3},{4,20},{20... | collective-permute-start | bytes 3145736 | tf_op jit(solution)/shard_map/ppermute | solution.py:139
  60.2 4.9 %copy-start.3 = (s32[2]{0:T(128)}, s32[2]{0:T(128)S(1)}, u32[]{:S(2)}) copy-start(s32[2]{0:T(128)S(1)} %pad_add_fusion.where_ref) | copy-start | bytes 28
  61.0 0.7 copy-start.2
  61.6 3.5 %collective-permute-start.3 = (bf16[384,256]{1,0:T(8,128)(2,1)S(1)}, bf16[384,256]{1,0:T(8,128)(2,1)S(1)}, u32[]{:S(2)}, u32[]{:S(2)}) collective-permute-start(bf16[384,256]{1,0:T(8,128)(2,1)S(1)} %get-tuple-element.26), channel_id=1, source_target_pairs={{0,16},{16,0},{1,17},{17,1},{2,18},{18,2},{3,19},{19,3},{4,20},{20... | collective-permute-start | bytes 589832 | tf_op jit(solution)/shard_map/ppermute | solution.py:139
  65.1 0.7 copy-start.6
  65.1 1.0 copy-start.5
  70.6 1.9 %copy-start.4 = (bf16[4,4,192,256]{3,2,1,0:T(8,128)(2,1)}, bf16[4,4,192,256]{3,2,1,0:T(8,128)(2,1)S(1)}, u32[]{:S(2)}) copy-start(bf16[4,4,192,256]{3,2,1,0:T(8,128)(2,1)S(1)} %all-to-all-done.near_w_ref) | copy-start | bytes 4718596
  70.6 6.9 %collective-permute-start.4 = (bf16[4,4,192,256]{3,2,1,0:T(8,128)(2,1)S(1)}, bf16[4,4,192,256]{3,2,1,0:T(8,128)(2,1)}, u32[]{:S(2)}, u32[]{:S(2)}) collective-permute-start(bf16[4,4,192,256]{3,2,1,0:T(8,128)(2,1)S(1)} %all-to-all-done.near_w_ref), channel_id=1, source_target_pairs={{0,16},{16,0},{1,17},{17,1},{2,18},{18,2},{3,19},{19,3},{4,20},{20... | collective-permute-start | bytes 4718600 | tf_op jit(solution)/shard_map/ppermute | solution.py:139
  72.5 25.2 %all-to-all-start.1 = ((bf16[4,4,192,256]{3,2,1,0:T(8,128)(2,1)}), bf16[4,4,192,256]{3,2,1,0:T(8,128)(2,1)S(1)}, u32[]{:S(2)}, u32[]{:S(2)}) async-start(bf16[4,4,192,256]{3,2,1,0:T(8,128)(2,1)} %shard_map.94), calls=%async_computation.2 | async-start | bytes 3145728 | tf_op jit(solution)/shard_map/all_to_all | solution.py:131
  77.5 61.3 %reduce-scatter.2.cloned.1.call-start = ((), (), s32[]{:S(2)}) async-start(), calls=%async_computation.4 | async-start | bytes 1179648 | tf_op jit(solution)/shard_map/reduce_scatter | solution.py:184
  83.4 39.2 %copy-start.7 = (bf16[256,384]{1,0:T(8,128)(2,1)S(1)}, bf16[256,384]{1,0:T(8,128)(2,1)}, u32[]{:S(2)}) copy-start(bf16[256,384]{1,0:T(8,128)(2,1)} %get-tuple-element.28) | copy-start | bytes 589828
  83.4 16.9 %collective-permute-start.5 = (bf16[256,384]{1,0:T(8,128)(2,1)}, bf16[256,384]{1,0:T(8,128)(2,1)S(1)}, u32[]{:S(2)}, u32[]{:S(2)}) collective-permute-start(bf16[256,384]{1,0:T(8,128)(2,1)} %get-tuple-element.29), channel_id=1, source_target_pairs={{0,1},{1,0},{2,3},{3,2},{4,5},{5,4},{6,7},{7,6},{8,9},{9,8},{10,11... | collective-permute-start | bytes 589832 | tf_op jit(solution)/shard_map/ppermute | solution.py:139
  114.7 13.5 %collective-permute-start.6 = (bf16[192,256]{1,0:T(8,128)(2,1)S(1)}, bf16[192,256]{1,0:T(8,128)(2,1)S(1)}, u32[]{:S(2)}, u32[]{:S(2)}) collective-permute-start(bf16[192,256]{1,0:T(8,128)(2,1)S(1)} %fusion), channel_id=1, source_target_pairs={{0,0},{2,64},{4,128},{6,192},{8,256},{10,320},{12,384},{14,448},{3... | collective-permute-start | bytes 294920 | tf_op jit(solution)/shard_map/ppermute | solution.py:122
Sparse Core Ops, SparseCore 0:
  10.7 47.5 all-gather.3
  83.5 55.3 reduce-scatter.1

commit v3 on v2

--- a/solution.py
+++ b/solution.py
@@ -86,26 +86,30 @@
         sum_ref[y] = sum(blocks_ref[x, y].astype(F32) for x in range(4)).astype(BF16)
 
 
-def project(
-    where_ref, ctx_ref, own_ref, far_ref, near_w_ref, far_w_ref,
-    dctx_ref, keep_ref, send_ref, weight, ctx
-):
-    core, half = where_ref[0], where_ref[1]
-    near_row = pl.multiple_of(core * STRIP, 16)
-    far_row = pl.multiple_of((1 - core) * STRIP, 16)
+def project_back(where_ref, mine_ref, theirs_ref, near_w_ref, far_w_ref, dctx_ref):
+    half = where_ref[1]
     for z in range(8):
-        cols = slice(z * 256, (z + 1) * 256)
-        ctx[:, cols] = ctx_ref[z]
+        part = None
         for slot in range(2):
             x = 2 * (z % 2) + (half if slot == 0 else 1 - half)
-            weight[slot, pl.ds(near_row, STRIP), cols] = near_w_ref[x, z // 2]
-            weight[slot, pl.ds(far_row, STRIP), cols] = far_w_ref[x, z // 2]
-    for z in range(8):
-        cols = slice(z * 256, (z + 1) * 256)
-        part = dot(own_ref[...], weight[0, :, cols], NN) + dot(far_ref[...], weight[1, :, cols], NN)
+            rows = slice(slot * STRIP, (slot + 1) * STRIP)
+            both = dot(mine_ref[rows, :], near_w_ref[x, z // 2], TN) + dot(
+                theirs_ref[rows, :], far_w_ref[x, z // 2], TN
+            )
+            part = both if part is None else part + both
         dctx_ref[z] = part.astype(BF16)
-    keep_ref[...] = dot(ctx[...], weight[0], NT).astype(BF16)
-    send_ref[...] = dot(ctx[...], weight[1], NT).astype(BF16)
+
+
+def project(where_ref, ctx_ref, near_w_ref, far_w_ref, keep_ref, send_ref):
+    core, half = where_ref[0], where_ref[1]
+    for slot, out_ref in enumerate((keep_ref, send_ref)):
+        x_lo = half if slot == 0 else 1 - half
+        mine, theirs = (
+            sum(dot(ctx_ref[z], w_ref[2 * (z % 2) + x_lo, z // 2], NT) for z in range(8)).astype(BF16)
+            for w_ref in (near_w_ref, far_w_ref)
+        )
+        out_ref[:, :STRIP] = jnp.where(core == 0, mine, theirs)
+        out_ref[:, STRIP:] = jnp.where(core == 0, theirs, mine)
 
 
 def plane_pairs():
@@ -164,31 +168,34 @@
     other_cot = swap(cot_theirs, "core")
     other_ctx = swap(ctx, "core")
     term = call(
-        weight_term, [((4, 4, STRIP, 256), BF16)], [], 2**29, 2**22, 4, True, vmem_mib=60
+        weight_term, [((4, 4, STRIP, 256), BF16)], [], 2**29, 2**22, 4, True, vmem_mib=10
     )(where, ctx, other_ctx, cot_mine, other_cot)[0]
     near, term = lax.optimization_barrier((near, term))
     far = swap(near, "core")
     term = scatter(term, "x")
     term = call(add_up, [((4, STRIP, 256), BF16)], [], 2**20, 2**21, 1, vmem_mib=4)(term)[0]
 
-    dctx, keep, send = call(
+    dctx = call(
+        project_back, [((8, 256, 256), BF16)], [], 2**29, 2**22, 4, True, vmem_mib=10
+    )(where, cot_mine, cot_theirs, near, far)[0]
+    dctx = lax.psum_scatter(dctx, "z", scatter_dimension=0, tiled=True)[0]
+    keep, send = call(
         project,
-        [((8, 256, 256), BF16), wide, wide],
-        [pltpu.VMEM((2, 384, 2048), BF16), pltpu.VMEM((256, 2048), BF16)],
-        2**30,
-        2**23,
-        5,
+        [wide, wide],
+        [],
+        2**29,
+        2**22,
+        3,
         True,
-        vmem_mib=60,
-    )(where, ctx, grad_out, far_cot, near, far)
-    dctx = lax.psum_scatter(dctx, "z", scatter_dimension=0, tiled=True)[0]
+        vmem_mib=12,
+    )(where, ctx, near, far)
     received = swap(send, "y_hi")
     layer_out = total([keep, received]).astype(BF16)
     term, received = lax.optimization_barrier((term, received))
     term = total(scatter(term, "y_lo")).astype(BF16)
     grad_weight = change_plane(term).T.astype(F32)
     grad_query, grad_key, grad_value = call(
-        attend_back, [square] * 3, [], 2**27, 2**21, 5, vmem_mib=60
+        attend_back, [square] * 3, [], 2**27, 2**21, 5, vmem_mib=6
     )(query_rows, key_rows, value_rows, probs, dctx)
     return (layer_out, grad_query, grad_key, grad_value, grad_weight)
 

time: 149 us -> 146 us (0.980)
  the two profiles are of different devices: /device:TPU:58 before, /device:TPU:56 now
where the time goes in v3:
time: 146 us; the launch traced here: 144 us
  starting transfers between devices  43.3 us (30%)
  blocking collectives  33.7 us (23%)
  waiting for transfers between devices  32.9 us (23%)
  between operations  14.2 us (10%)
  Pallas kernels  13.1 us (9%)
  local copies, waits for them, and re-layouts  5.67 us (4%)
  other arithmetic  1.55 us (1%)
    ppermute x2, starting transfers between devices, change_plane(): return lax.ppermute(block, ('y_lo', 'x', 'z'), plane_pairs())  20.6 us
    all_gather x1, blocking collectives, local(): weight = lax.all_gather(weight, 'y_lo', axis=0)  18.9 us
    all_to_all x1, blocking collectives, scatter(): return lax.all_to_all(blocks, axis, split_axis=0, concat_axis=0, tiled=True)  14.8 us
    ppermute x5, starting transfers between devices, swap(): return lax.ppermute(block, axis, [(0, 1), (1, 0)])  12 us
    all_to_all x1, waiting for transfers between devices, scatter(): return lax.all_to_all(blocks, axis, split_axis=0, concat_axis=0, tiled=True)  11.8 us
    ppermute x2, waiting for transfers between devices, change_plane(): return lax.ppermute(block, ('y_lo', 'x', 'z'), plane_pairs())  10.7 us
    all_to_all x1, starting transfers between devices, gather(): return lax.all_to_all(wide, axis, split_axis=0, concat_axis=0, tiled=True)  6.24 us
    reduce_scatter x1, waiting for transfers between devices, local(): dctx = lax.psum_scatter(dctx, 'z', scatter_dimension=0, tiled=True)[0]  4.54 us
  transfers between devices with their start and end apart: 11, of which 7 were waited for; matrix products, arithmetic and copies ran while one was open for 2% of the time, Pallas kernels for 6%

profile of v3, /device:TPU:56, one launch (start us, length us, event | category | flops | bytes accessed | tf_op | source)
XLA Modules:
  0.0 144.4 jit_solution(8011778308452075758)
XLA Ops:
  7.2 0.0 all-gather.4.cloned.1.call-start
  7.2 2.7 %shard_map.92 = (bf16[256,256]{1,0:T(8,128)(2,1)}, f32[2,256,256]{2,1,0:T(8,128)}) custom-call(bf16[256,256]{1,0:T(8,128)(2,1)} %q_ref.3, bf16[256,256]{1,0:T(8,128)(2,1)} %k_ref.3, bf16[256,256]{1,0:T(8,128)(2,1)} %v_ref.3), custom_call_target="tpu_custom_call" | custom-call | flops 67108864 | bytes 1048576 | tf_op jit(solution)/shard_map/pallas_call | solution.py:152
  9.9 0.0 all-gather.4.cloned.1.call-update
  9.9 13.3 %collective-permute-start = (bf16[192,256]{1,0:T(8,128)(2,1)}, bf16[192,256]{1,0:T(8,128)(2,1)S(1)}, u32[]{:S(2)}, u32[]{:S(2)}) collective-permute-start(bf16[192,256]{1,0:T(8,128)(2,1)} %bitcast.15), channel_id=1, source_target_pairs={{0,0},{2,64},{4,128},{6,192},{8,256},{10,320},{12,384},{14,448},{3... | collective-permute-start | bytes 294920 | tf_op jit(solution)/shard_map/ppermute | solution.py:126
  23.2 2.0 %collective-permute-start.1 = (bf16[256,384]{1,0:T(8,128)(2,1)}, bf16[256,384]{1,0:T(8,128)(2,1)S(1)}, u32[]{:S(2)}, u32[]{:S(2)}) collective-permute-start(bf16[256,384]{1,0:T(8,128)(2,1)} %own_ref), channel_id=1, source_target_pairs={{0,1},{1,0},{2,3},{3,2},{4,5},{5,4},{6,7},{7,6},{8,9},{9,8},{10,11... | collective-permute-start | bytes 589832 | tf_op jit(solution)/shard_map/ppermute | solution.py:143
  25.2 5.0 %collective-permute-done = bf16[192,256]{1,0:T(8,128)(2,1)S(1)} collective-permute-done((bf16[192,256]{1,0:T(8,128)(2,1)}, bf16[192,256]{1,0:T(8,128)(2,1)S(1)}, u32[]{:S(2)}, u32[]{:S(2)}) %collective-permute-start) | collective-permute-done | bytes 98336 | tf_op jit(solution)/shard_map/ppermute | solution.py:126
  30.2 18.9 %all-gather.1 = bf16[768,256]{1,0:T(8,128)(2,1)S(1)} all-gather(bf16[192,256]{1,0:T(8,128)(2,1)S(1)} %collective-permute-done), channel_id=3, replica_groups=mesh['y_lo'=4,'x'=4,'core'=2,'z'=8,'y_hi'=2] {'y_lo'}, dimensions={0}, use_global_device_ids=true | all-gather | bytes 491520 | tf_op jit(solution)/shard_map/all_gather | solution.py:160
  49.1 0.0 collective-permute-done.1.far_ref
  49.1 1.3 broadcast_in_dim.2
  50.4 0.0 copy-start.7
  50.4 6.2 %all-to-all-start = ((bf16[4,4,192,256]{3,2,1,0:T(8,128)(2,1)}), bf16[4,4,192,256]{3,2,1,0:T(8,128)(2,1)S(1)}, u32[]{:S(2)}, u32[]{:S(2)}) async-start(bf16[4,4,192,256]{3,2,1,0:T(8,128)(2,1)} %broadcast_in_dim.2), calls=%async_computation | async-start | bytes 3145728 | tf_op jit(solution)/shard_map/all_to_all | solution.py:131
  56.7 1.6 %all-gather.4.cloned.1.call-done = bf16[2048,256]{1,0:T(8,128)(2,1)} async-done(((bf16[256,256]{1,0:T(8,128)(2,1)}), bf16[2048,256]{1,0:T(8,128)(2,1)}) %all-gather.4.cloned.1.call-update) | async-done | bytes 1048592 | tf_op jit(solution)/shard_map/all_gather | solution.py:155
  58.3 1.9 %collective-permute-start.2 = (bf16[8,256,256]{2,1,0:T(8,128)(2,1)}, bf16[8,256,256]{2,1,0:T(8,128)(2,1)S(1)}, u32[]{:S(2)}, u32[]{:S(2)}) collective-permute-start(bf16[8,256,256]{2,1,0:T(8,128)(2,1)} %bitcast.10), channel_id=1, source_target_pairs={{0,16},{16,0},{1,17},{17,1},{2,18},{18,2},{3,19},{19,3},{4,20},{20... | collective-permute-start | bytes 3145736 | tf_op jit(solution)/shard_map/ppermute | solution.py:143
  60.2 0.1 pad_add_fusion.where_ref
  60.3 0.0 copy-done.7
  60.3 0.7 shard_map.93
  61.0 2.4 %collective-permute-start.3 = (bf16[384,256]{1,0:T(8,128)(2,1)S(1)}, bf16[384,256]{1,0:T(8,128)(2,1)S(1)}, u32[]{:S(2)}, u32[]{:S(2)}) collective-permute-start(bf16[384,256]{1,0:T(8,128)(2,1)S(1)} %get-tuple-element.25.theirs_ref), channel_id=1, source_target_pairs={{0,16},{16,0},{1,17},{17,1},{2,18},{18,2},{3,19},{19,3},{4,20},{20... | collective-permute-start | bytes 589832 | tf_op jit(solution)/shard_map/ppermute | solution.py:143
  63.5 1.0 collective-permute-done.3.other_cot_ref
  64.5 0.0 collective-permute-done.2.other_ctx_ref
  64.5 0.0 copy-start.1
  64.5 1.2 copy-done.1
  65.7 2.8 %shard_map.94 = bf16[4,4,192,256]{3,2,1,0:T(8,128)(2,1)} custom-call(s32[2]{0:T(128)S(1)} %pad_add_fusion.where_ref, bf16[8,256,256]{2,1,0:T(8,128)(2,1)S(1)} %bitcast.11, bf16[8,256,256]{2,1,0:T(8,128)(2,1)S(1)} %collective-permute-done.2.other_ctx_ref, bf16[384,256]{1,0:T(8,128)(2,1)S(1)} %get-tuple-element.24.cot_ref.mine_ref, ...), custom_call_target="tpu_custom_call" | custom-call | flops 536870912 | bytes 4194304 | tf_op jit(solution)/shard_map/pallas_call | solution.py:170
  68.5 3.0 %all-to-all-done.near_w_ref = bf16[4,4,192,256]{3,2,1,0:T(8,128)(2,1)S(1)} async-done(((bf16[4,4,192,256]{3,2,1,0:T(8,128)(2,1)}), bf16[4,4,192,256]{3,2,1,0:T(8,128)(2,1)S(1)}, u32[]{:S(2)}, u32[]{:S(2)}) %all-to-all-start) | async-done | bytes 1572896 | tf_op jit(solution)/shard_map/all_to_all | solution.py:131
  71.5 1.9 %collective-permute-start.4 = (bf16[4,4,192,256]{3,2,1,0:T(8,128)(2,1)S(1)}, bf16[4,4,192,256]{3,2,1,0:T(8,128)(2,1)S(1)}, u32[]{:S(2)}, u32[]{:S(2)}) collective-permute-start(bf16[4,4,192,256]{3,2,1,0:T(8,128)(2,1)S(1)} %all-to-all-done.near_w_ref), channel_id=1, source_target_pairs={{0,16},{16,0},{1,17},{17,1},{2,18},{18,2},{3,19},{19,3},{4,20},{20... | collective-permute-start | bytes 4718600 | tf_op jit(solution)/shard_map/ppermute | solution.py:143
  73.5 4.4 %all-to-all-start.1 = ((bf16[4,4,192,256]{3,2,1,0:T(8,128)(2,1)}), bf16[4,4,192,256]{3,2,1,0:T(8,128)(2,1)}, u32[]{:S(2)}, u32[]{:S(2)}) async-start(bf16[4,4,192,256]{3,2,1,0:T(8,128)(2,1)} %shard_map.94), calls=%async_computation.2 | async-start | bytes 3145728 | tf_op jit(solution)/shard_map/all_to_all | solution.py:135
  77.9 0.0 reduce-scatter.2.cloned.1.call-start
  77.9 0.0 collective-permute-done.4.far_w_ref
  77.9 1.9 %shard_map.96 = bf16[8,256,256]{2,1,0:T(8,128)(2,1)S(1)} custom-call(s32[2]{0:T(128)S(1)} %pad_add_fusion.where_ref, bf16[384,256]{1,0:T(8,128)(2,1)S(1)} %get-tuple-element.24.cot_ref.mine_ref, bf16[384,256]{1,0:T(8,128)(2,1)S(1)} %get-tuple-element.25.theirs_ref, bf16[4,4,192,256]{3,2,1,0:T(8,128)(2,1)S(1)} %all-to-all-done.near_w_ref, ...), custom_call_target="tpu_custom_call" | custom-call | flops 536870912 | bytes 4194304 | tf_op jit(solution)/shard_map/pallas_call | solution.py:178
  79.8 0.0 copy-start
  79.8 1.0 copy-done
  80.8 0.0 reduce-scatter.2.cloned.1.call-update
  80.8 0.0 copy-start.2
  80.8 1.2 copy-done.2
  82.0 1.9 %shard_map.95 = (bf16[256,384]{1,0:T(8,128)(2,1)S(1)}, bf16[256,384]{1,0:T(8,128)(2,1)S(1)}) custom-call(s32[2]{0:T(128)S(1)} %pad_add_fusion.where_ref, bf16[8,256,256]{2,1,0:T(8,128)(2,1)S(1)} %bitcast.12, bf16[4,4,192,256]{3,2,1,0:T(8,128)(2,1)S(1)} %all-to-all-done.near_w_ref, bf16[4,4,192,256]{3,2,1,0:T(8,128)(2,1)S(1)} %collective-permute-done.4.far_w_ref), custom_call_target="tpu_custom_call" | custom-call | flops 536870912 | bytes 4194304 | tf_op jit(solution)/shard_map/pallas_call | solution.py:182
  83.9 3.8 %collective-permute-start.5 = (bf16[256,384]{1,0:T(8,128)(2,1)S(1)}, bf16[256,384]{1,0:T(8,128)(2,1)S(1)}, u32[]{:S(2)}, u32[]{:S(2)}) collective-permute-start(bf16[256,384]{1,0:T(8,128)(2,1)S(1)} %get-tuple-element.28), channel_id=1, source_target_pairs={{0,1},{1,0},{2,3},{3,2},{4,5},{5,4},{6,7},{7,6},{8,9},{9,8},{10,11... | collective-permute-start | bytes 589832 | tf_op jit(solution)/shard_map/ppermute | solution.py:143
  87.7 11.8 %all-to-all-done.1.blocks_ref = bf16[4,4,192,256]{3,2,1,0:T(8,128)(2,1)} async-done(((bf16[4,4,192,256]{3,2,1,0:T(8,128)(2,1)}), bf16[4,4,192,256]{3,2,1,0:T(8,128)(2,1)}, u32[]{:S(2)}, u32[]{:S(2)}) %all-to-all-start.1) | async-done | bytes 1572896 | tf_op jit(solution)/shard_map/all_to_all | solution.py:135
  99.6 1.6 %shard_map.98 = bf16[4,192,256]{2,1,0:T(8,128)(2,1)S(1)} custom-call(bf16[4,4,192,256]{3,2,1,0:T(8,128)(2,1)} %all-to-all-done.1.blocks_ref), custom_call_target="tpu_custom_call" | custom-call | flops 1048576 | bytes 2097152 | tf_op jit(solution)/shard_map/pallas_call | solution.py:176
  101.2 0.0 copy-start.3
  101.2 0.0 copy-start.4
  101.2 0.0 copy-start.5
  101.2 0.0 copy-start.6
  101.2 0.0 collective-permute-done.5
  101.2 14.8 %all_to_all.15 = bf16[4,192,256]{2,1,0:T(8,128)(2,1)S(1)} all-to-all(bf16[4,192,256]{2,1,0:T(8,128)(2,1)S(1)} %shard_map.98), channel_id=1, replica_groups=mesh['y_lo'=4,'x'=4,'core'=2,'z'=8,'y_hi'=2] {'y_lo'}, dimensions={0} | all-to-all | bytes 786432 | tf_op jit(solution)/shard_map/all_to_all | solution.py:135
  116.0 0.1 fusion
  116.1 7.3 %collective-permute-start.6 = (bf16[192,256]{1,0:T(8,128)(2,1)S(1)}, bf16[192,256]{1,0:T(8,128)(2,1)S(1)}, u32[]{:S(2)}, u32[]{:S(2)}) collective-permute-start(bf16[192,256]{1,0:T(8,128)(2,1)S(1)} %fusion), channel_id=1, source_target_pairs={{0,0},{2,64},{4,128},{6,192},{8,256},{10,320},{12,384},{14,448},{3... | collective-permute-start | bytes 294920 | tf_op jit(solution)/shard_map/ppermute | solution.py:126
  123.4 0.7 add_convert_fusion
  124.1 5.7 %collective-permute-done.6 = bf16[192,256]{1,0:T(8,128)(2,1)S(1)} collective-permute-done((bf16[192,256]{1,0:T(8,128)(2,1)S(1)}, bf16[192,256]{1,0:T(8,128)(2,1)S(1)}, u32[]{:S(2)}, u32[]{:S(2)}) %collective-permute-start.6) | collective-permute-done | bytes 98336 | tf_op jit(solution)/shard_map/ppermute | solution.py:126
  129.8 0.7 convert_bitcast_fusion
  130.5 4.5 %reduce-scatter.2.cloned.1.call-done = bf16[1,256,256]{2,1,0:T(8,128)(2,1)} async-done(((bf16[8,256,256]{2,1,0:T(8,128)(2,1)}), bf16[1,256,256]{2,1,0:T(8,128)(2,1)}) %reduce-scatter.2.cloned.1.call-update) | async-done | bytes 131088 | tf_op jit(solution)/shard_map/reduce_scatter | solution.py:181
  135.0 0.0 copy-done.3
  135.0 0.0 copy-done.4
  135.0 0.0 copy-done.5
  135.0 0.0 copy-done.6
  135.1 0.0 copy-start.8
  135.1 0.9 copy-done.8
  136.0 1.6 %shard_map.97 = (bf16[256,256]{1,0:T(8,128)(2,1)}, bf16[256,256]{1,0:T(8,128)(2,1)}, bf16[256,256]{1,0:T(8,128)(2,1)}) custom-call(bf16[256,256]{1,0:T(8,128)(2,1)S(1)} %copy-done.4, bf16[256,256]{1,0:T(8,128)(2,1)S(1)} %copy-done.5, bf16[256,256]{1,0:T(8,128)(2,1)S(1)} %copy-done.6, f32[2,256,256]{2,1,0:T(8,128)S(1)} %copy-done.3, bf16[256,256]{1,0:T(8,128)(2,1)S(1)} %bitcast.13), custom_call_target="tpu_custom_call" | custom-call | flops 134217728 | bytes 2097152 | tf_op jit(solution)/shard_map/pallas_call | solution.py:197
Async XLA Ops:
  7.2 51.1 %all-gather.4.cloned.1.call-start = ((), (), s32[]{:S(2)}) async-start(), calls=%async_computation.5 | async-start | bytes 1179648 | tf_op jit(solution)/shard_map/all_gather | solution.py:155
  9.9 20.3 %collective-permute-start = (bf16[192,256]{1,0:T(8,128)(2,1)}, bf16[192,256]{1,0:T(8,128)(2,1)S(1)}, u32[]{:S(2)}, u32[]{:S(2)}) collective-permute-start(bf16[192,256]{1,0:T(8,128)(2,1)} %bitcast.15), channel_id=1, source_target_pairs={{0,0},{2,64},{4,128},{6,192},{8,256},{10,320},{12,384},{14,448},{3... | collective-permute-start | bytes 294920 | tf_op jit(solution)/shard_map/ppermute | solution.py:126
  23.2 25.9 %collective-permute-start.1 = (bf16[256,384]{1,0:T(8,128)(2,1)}, bf16[256,384]{1,0:T(8,128)(2,1)S(1)}, u32[]{:S(2)}, u32[]{:S(2)}) collective-permute-start(bf16[256,384]{1,0:T(8,128)(2,1)} %own_ref), channel_id=1, source_target_pairs={{0,1},{1,0},{2,3},{3,2},{4,5},{5,4},{6,7},{7,6},{8,9},{9,8},{10,11... | collective-permute-start | bytes 589832 | tf_op jit(solution)/shard_map/ppermute | solution.py:143
  50.4 9.9 %copy-start.7 = (bf16[256,384]{1,0:T(8,128)(2,1)S(1)}, bf16[256,384]{1,0:T(8,128)(2,1)}, u32[]{:S(2)}) copy-start(bf16[256,384]{1,0:T(8,128)(2,1)} %own_ref) | copy-start | bytes 589828
  50.4 21.1 %all-to-all-start = ((bf16[4,4,192,256]{3,2,1,0:T(8,128)(2,1)}), bf16[4,4,192,256]{3,2,1,0:T(8,128)(2,1)S(1)}, u32[]{:S(2)}, u32[]{:S(2)}) async-start(bf16[4,4,192,256]{3,2,1,0:T(8,128)(2,1)} %broadcast_in_dim.2), calls=%async_computation | async-start | bytes 3145728 | tf_op jit(solution)/shard_map/all_to_all | solution.py:131
  58.3 6.2 %collective-permute-start.2 = (bf16[8,256,256]{2,1,0:T(8,128)(2,1)}, bf16[8,256,256]{2,1,0:T(8,128)(2,1)S(1)}, u32[]{:S(2)}, u32[]{:S(2)}) collective-permute-start(bf16[8,256,256]{2,1,0:T(8,128)(2,1)} %bitcast.10), channel_id=1, source_target_pairs={{0,16},{16,0},{1,17},{17,1},{2,18},{18,2},{3,19},{19,3},{4,20},{20... | collective-permute-start | bytes 3145736 | tf_op jit(solution)/shard_map/ppermute | solution.py:143
  61.0 3.5 %collective-permute-start.3 = (bf16[384,256]{1,0:T(8,128)(2,1)S(1)}, bf16[384,256]{1,0:T(8,128)(2,1)S(1)}, u32[]{:S(2)}, u32[]{:S(2)}) collective-permute-start(bf16[384,256]{1,0:T(8,128)(2,1)S(1)} %get-tuple-element.25.theirs_ref), channel_id=1, source_target_pairs={{0,16},{16,0},{1,17},{17,1},{2,18},{18,2},{3,19},{19,3},{4,20},{20... | collective-permute-start | bytes 589832 | tf_op jit(solution)/shard_map/ppermute | solution.py:143
  64.5 1.2 copy-start.1
  71.5 6.4 %collective-permute-start.4 = (bf16[4,4,192,256]{3,2,1,0:T(8,128)(2,1)S(1)}, bf16[4,4,192,256]{3,2,1,0:T(8,128)(2,1)S(1)}, u32[]{:S(2)}, u32[]{:S(2)}) collective-permute-start(bf16[4,4,192,256]{3,2,1,0:T(8,128)(2,1)S(1)} %all-to-all-done.near_w_ref), channel_id=1, source_target_pairs={{0,16},{16,0},{1,17},{17,1},{2,18},{18,2},{3,19},{19,3},{4,20},{20... | collective-permute-start | bytes 4718600 | tf_op jit(solution)/shard_map/ppermute | solution.py:143
  73.5 26.1 %all-to-all-start.1 = ((bf16[4,4,192,256]{3,2,1,0:T(8,128)(2,1)}), bf16[4,4,192,256]{3,2,1,0:T(8,128)(2,1)}, u32[]{:S(2)}, u32[]{:S(2)}) async-start(bf16[4,4,192,256]{3,2,1,0:T(8,128)(2,1)} %shard_map.94), calls=%async_computation.2 | async-start | bytes 3145728 | tf_op jit(solution)/shard_map/all_to_all | solution.py:135
  77.9 57.2 %reduce-scatter.2.cloned.1.call-start = ((), (), s32[]{:S(2)}) async-start(), calls=%async_computation.4 | async-start | bytes 1179648 | tf_op jit(solution)/shard_map/reduce_scatter | solution.py:181
  79.8 1.0 copy-start
  80.8 1.2 copy-start.2
  83.9 17.3 %collective-permute-start.5 = (bf16[256,384]{1,0:T(8,128)(2,1)S(1)}, bf16[256,384]{1,0:T(8,128)(2,1)S(1)}, u32[]{:S(2)}, u32[]{:S(2)}) collective-permute-start(bf16[256,384]{1,0:T(8,128)(2,1)S(1)} %get-tuple-element.28), channel_id=1, source_target_pairs={{0,1},{1,0},{2,3},{3,2},{4,5},{5,4},{6,7},{7,6},{8,9},{9,8},{10,11... | collective-permute-start | bytes 589832 | tf_op jit(solution)/shard_map/ppermute | solution.py:143
  101.2 33.9 %copy-start.3 = (f32[2,256,256]{2,1,0:T(8,128)S(1)}, f32[2,256,256]{2,1,0:T(8,128)}, u32[]{:S(2)}) copy-start(f32[2,256,256]{2,1,0:T(8,128)} %get-tuple-element.29.probs_ref) | copy-start | bytes 1572868
  101.2 33.8 %copy-start.4 = (bf16[256,256]{1,0:T(8,128)(2,1)S(1)}, bf16[256,256]{1,0:T(8,128)(2,1)}, u32[]{:S(2)}) copy-start(bf16[256,256]{1,0:T(8,128)(2,1)} %q_ref.3) | copy-start | bytes 393220
  101.2 33.8 %copy-start.5 = (bf16[256,256]{1,0:T(8,128)(2,1)S(1)}, bf16[256,256]{1,0:T(8,128)(2,1)}, u32[]{:S(2)}) copy-start(bf16[256,256]{1,0:T(8,128)(2,1)} %k_ref.3) | copy-start | bytes 393220
  101.2 33.8 %copy-start.6 = (bf16[256,256]{1,0:T(8,128)(2,1)S(1)}, bf16[256,256]{1,0:T(8,128)(2,1)}, u32[]{:S(2)}) copy-start(bf16[256,256]{1,0:T(8,128)(2,1)} %v_ref.3) | copy-start | bytes 393220
  116.1 13.7 %collective-permute-start.6 = (bf16[192,256]{1,0:T(8,128)(2,1)S(1)}, bf16[192,256]{1,0:T(8,128)(2,1)S(1)}, u32[]{:S(2)}, u32[]{:S(2)}) collective-permute-start(bf16[192,256]{1,0:T(8,128)(2,1)S(1)} %fusion), channel_id=1, source_target_pairs={{0,0},{2,64},{4,128},{6,192},{8,256},{10,320},{12,384},{14,448},{3... | collective-permute-start | bytes 294920 | tf_op jit(solution)/shard_map/ppermute | solution.py:126
  135.1 0.9 copy-start.8
Sparse Core Ops, SparseCore 0:
  10.7 47.6 all-gather.3
  81.5 53.4 reduce-scatter.1

commit v4 on v3

--- a/solution.py
+++ b/solution.py
@@ -193,10 +193,12 @@
     layer_out = total([keep, received]).astype(BF16)
     term, received = lax.optimization_barrier((term, received))
     term = total(scatter(term, "y_lo")).astype(BF16)
-    grad_weight = change_plane(term).T.astype(F32)
+    term = change_plane(term)
     grad_query, grad_key, grad_value = call(
         attend_back, [square] * 3, [], 2**27, 2**21, 5, vmem_mib=6
     )(query_rows, key_rows, value_rows, probs, dctx)
+    term, grad_query = lax.optimization_barrier((term, grad_query))
+    grad_weight = term.T.astype(F32)
     return (layer_out, grad_query, grad_key, grad_value, grad_weight)
 
 

time: 146 us -> 146 us (level)
    reduce_scatter x1, waiting for transfers between devices: 4.54 us -> 11 us  [local(): dctx = lax.psum_scatter(dctx, 'z', scatter_dimension=0, tiled=True)[0]]
    ppermute x2, waiting for transfers between devices: 10.7 us -> 5 us  [change_plane(): return lax.ppermute(block, ('y_lo', 'x', 'z'), plane_pairs())]
  transfers between devices with their start and end apart: 11 -> 11, of which waited for: 7 -> 6; matrix products, arithmetic and copies ran while one was open for 2% -> 1% of each run, Pallas kernels for 6% -> 7%
where the time goes in v4:
time: 146 us; the launch traced here: 145 us
  starting transfers between devices  43.7 us (30%)
  blocking collectives  33.5 us (23%)
  waiting for transfers between devices  33.4 us (23%)
  between operations  14.2 us (10%)
  Pallas kernels  13.1 us (9%)
  local copies, waits for them, and re-layouts  5.67 us (4%)
  other arithmetic  1.55 us (1%)
    ppermute x2, starting transfers between devices, change_plane(): return lax.ppermute(block, ('y_lo', 'x', 'z'), plane_pairs())  20.8 us
    all_gather x1, blocking collectives, local(): weight = lax.all_gather(weight, 'y_lo', axis=0)  18.9 us
    all_to_all x1, blocking collectives, scatter(): return lax.all_to_all(blocks, axis, split_axis=0, concat_axis=0, tiled=True)  14.7 us
    ppermute x5, starting transfers between devices, swap(): return lax.ppermute(block, axis, [(0, 1), (1, 0)])  12.2 us
    all_to_all x1, waiting for transfers between devices, scatter(): return lax.all_to_all(blocks, axis, split_axis=0, concat_axis=0, tiled=True)  11.7 us
    reduce_scatter x1, waiting for transfers between devices, local(): dctx = lax.psum_scatter(dctx, 'z', scatter_dimension=0, tiled=True)[0]  11 us
    all_to_all x1, starting transfers between devices, gather(): return lax.all_to_all(wide, axis, split_axis=0, concat_axis=0, tiled=True)  6.24 us
    ppermute x2, waiting for transfers between devices, change_plane(): return lax.ppermute(block, ('y_lo', 'x', 'z'), plane_pairs())  5 us
  transfers between devices with their start and end apart: 11, of which 6 were waited for; matrix products, arithmetic and copies ran while one was open for 1% of the time, Pallas kernels for 7%

profile of v4, /device:TPU:56, one launch (start us, length us, event | category | flops | bytes accessed | tf_op | source)
XLA Modules:
  0.0 145.2 jit_solution(9847494432941771575)
XLA Ops:
  7.2 0.0 all-gather.4.cloned.1.call-start
  7.2 2.7 %shard_map.92 = (bf16[256,256]{1,0:T(8,128)(2,1)}, f32[2,256,256]{2,1,0:T(8,128)}) custom-call(bf16[256,256]{1,0:T(8,128)(2,1)} %q_ref.3, bf16[256,256]{1,0:T(8,128)(2,1)} %k_ref.3, bf16[256,256]{1,0:T(8,128)(2,1)} %v_ref.3), custom_call_target="tpu_custom_call" | custom-call | flops 67108864 | bytes 1048576 | tf_op jit(solution)/shard_map/pallas_call | solution.py:152
  9.9 0.0 all-gather.4.cloned.1.call-update
  9.9 13.3 %collective-permute-start = (bf16[192,256]{1,0:T(8,128)(2,1)}, bf16[192,256]{1,0:T(8,128)(2,1)S(1)}, u32[]{:S(2)}, u32[]{:S(2)}) collective-permute-start(bf16[192,256]{1,0:T(8,128)(2,1)} %bitcast.15), channel_id=1, source_target_pairs={{0,0},{2,64},{4,128},{6,192},{8,256},{10,320},{12,384},{14,448},{3... | collective-permute-start | bytes 294920 | tf_op jit(solution)/shard_map/ppermute | solution.py:126
  23.2 2.0 %collective-permute-start.1 = (bf16[256,384]{1,0:T(8,128)(2,1)}, bf16[256,384]{1,0:T(8,128)(2,1)S(1)}, u32[]{:S(2)}, u32[]{:S(2)}) collective-permute-start(bf16[256,384]{1,0:T(8,128)(2,1)} %own_ref), channel_id=1, source_target_pairs={{0,1},{1,0},{2,3},{3,2},{4,5},{5,4},{6,7},{7,6},{8,9},{9,8},{10,11... | collective-permute-start | bytes 589832 | tf_op jit(solution)/shard_map/ppermute | solution.py:143
  25.2 5.0 %collective-permute-done = bf16[192,256]{1,0:T(8,128)(2,1)S(1)} collective-permute-done((bf16[192,256]{1,0:T(8,128)(2,1)}, bf16[192,256]{1,0:T(8,128)(2,1)S(1)}, u32[]{:S(2)}, u32[]{:S(2)}) %collective-permute-start) | collective-permute-done | bytes 98336 | tf_op jit(solution)/shard_map/ppermute | solution.py:126
  30.2 18.9 %all-gather.1 = bf16[768,256]{1,0:T(8,128)(2,1)S(1)} all-gather(bf16[192,256]{1,0:T(8,128)(2,1)S(1)} %collective-permute-done), channel_id=3, replica_groups=mesh['y_lo'=4,'x'=4,'core'=2,'z'=8,'y_hi'=2] {'y_lo'}, dimensions={0}, use_global_device_ids=true | all-gather | bytes 491520 | tf_op jit(solution)/shard_map/all_gather | solution.py:160
  49.1 0.0 collective-permute-done.1.far_ref
  49.1 1.3 broadcast_in_dim.2
  50.4 0.0 copy-start.7
  50.4 6.2 %all-to-all-start = ((bf16[4,4,192,256]{3,2,1,0:T(8,128)(2,1)}), bf16[4,4,192,256]{3,2,1,0:T(8,128)(2,1)S(1)}, u32[]{:S(2)}, u32[]{:S(2)}) async-start(bf16[4,4,192,256]{3,2,1,0:T(8,128)(2,1)} %broadcast_in_dim.2), calls=%async_computation | async-start | bytes 3145728 | tf_op jit(solution)/shard_map/all_to_all | solution.py:131
  56.7 1.6 %all-gather.4.cloned.1.call-done = bf16[2048,256]{1,0:T(8,128)(2,1)} async-done(((bf16[256,256]{1,0:T(8,128)(2,1)}), bf16[2048,256]{1,0:T(8,128)(2,1)}) %all-gather.4.cloned.1.call-update) | async-done | bytes 1048592 | tf_op jit(solution)/shard_map/all_gather | solution.py:155
  58.3 1.9 %collective-permute-start.2 = (bf16[8,256,256]{2,1,0:T(8,128)(2,1)}, bf16[8,256,256]{2,1,0:T(8,128)(2,1)S(1)}, u32[]{:S(2)}, u32[]{:S(2)}) collective-permute-start(bf16[8,256,256]{2,1,0:T(8,128)(2,1)} %bitcast.10), channel_id=1, source_target_pairs={{0,16},{16,0},{1,17},{17,1},{2,18},{18,2},{3,19},{19,3},{4,20},{20... | collective-permute-start | bytes 3145736 | tf_op jit(solution)/shard_map/ppermute | solution.py:143
  60.2 0.1 pad_add_fusion.where_ref
  60.3 0.0 copy-done.7
  60.3 0.7 shard_map.93
  61.0 2.4 %collective-permute-start.3 = (bf16[384,256]{1,0:T(8,128)(2,1)S(1)}, bf16[384,256]{1,0:T(8,128)(2,1)S(1)}, u32[]{:S(2)}, u32[]{:S(2)}) collective-permute-start(bf16[384,256]{1,0:T(8,128)(2,1)S(1)} %get-tuple-element.27.theirs_ref), channel_id=1, source_target_pairs={{0,16},{16,0},{1,17},{17,1},{2,18},{18,2},{3,19},{19,3},{4,20},{20... | collective-permute-start | bytes 589832 | tf_op jit(solution)/shard_map/ppermute | solution.py:143
  63.5 1.0 collective-permute-done.3.other_cot_ref
  64.5 0.0 collective-permute-done.2.other_ctx_ref
  64.5 0.0 copy-start.1
  64.5 1.2 copy-done.1
  65.7 2.8 %shard_map.94 = bf16[4,4,192,256]{3,2,1,0:T(8,128)(2,1)} custom-call(s32[2]{0:T(128)S(1)} %pad_add_fusion.where_ref, bf16[8,256,256]{2,1,0:T(8,128)(2,1)S(1)} %bitcast.11, bf16[8,256,256]{2,1,0:T(8,128)(2,1)S(1)} %collective-permute-done.2.other_ctx_ref, bf16[384,256]{1,0:T(8,128)(2,1)S(1)} %get-tuple-element.26.cot_ref.mine_ref, ...), custom_call_target="tpu_custom_call" | custom-call | flops 536870912 | bytes 4194304 | tf_op jit(solution)/shard_map/pallas_call | solution.py:170
  68.5 3.0 %all-to-all-done.near_w_ref = bf16[4,4,192,256]{3,2,1,0:T(8,128)(2,1)S(1)} async-done(((bf16[4,4,192,256]{3,2,1,0:T(8,128)(2,1)}), bf16[4,4,192,256]{3,2,1,0:T(8,128)(2,1)S(1)}, u32[]{:S(2)}, u32[]{:S(2)}) %all-to-all-start) | async-done | bytes 1572896 | tf_op jit(solution)/shard_map/all_to_all | solution.py:131
  71.5 1.9 %collective-permute-start.4 = (bf16[4,4,192,256]{3,2,1,0:T(8,128)(2,1)S(1)}, bf16[4,4,192,256]{3,2,1,0:T(8,128)(2,1)S(1)}, u32[]{:S(2)}, u32[]{:S(2)}) collective-permute-start(bf16[4,4,192,256]{3,2,1,0:T(8,128)(2,1)S(1)} %all-to-all-done.near_w_ref), channel_id=1, source_target_pairs={{0,16},{16,0},{1,17},{17,1},{2,18},{18,2},{3,19},{19,3},{4,20},{20... | collective-permute-start | bytes 4718600 | tf_op jit(solution)/shard_map/ppermute | solution.py:143
  73.5 4.4 %all-to-all-start.1 = ((bf16[4,4,192,256]{3,2,1,0:T(8,128)(2,1)}), bf16[4,4,192,256]{3,2,1,0:T(8,128)(2,1)}, u32[]{:S(2)}, u32[]{:S(2)}) async-start(bf16[4,4,192,256]{3,2,1,0:T(8,128)(2,1)} %shard_map.94), calls=%async_computation.1 | async-start | bytes 3145728 | tf_op jit(solution)/shard_map/all_to_all | solution.py:135
  77.9 0.0 reduce-scatter.2.cloned.1.call-start
  77.9 0.0 collective-permute-done.4.far_w_ref
  77.9 1.9 %shard_map.97 = bf16[8,256,256]{2,1,0:T(8,128)(2,1)S(1)} custom-call(s32[2]{0:T(128)S(1)} %pad_add_fusion.where_ref, bf16[384,256]{1,0:T(8,128)(2,1)S(1)} %get-tuple-element.26.cot_ref.mine_ref, bf16[384,256]{1,0:T(8,128)(2,1)S(1)} %get-tuple-element.27.theirs_ref, bf16[4,4,192,256]{3,2,1,0:T(8,128)(2,1)S(1)} %all-to-all-done.near_w_ref, ...), custom_call_target="tpu_custom_call" | custom-call | flops 536870912 | bytes 4194304 | tf_op jit(solution)/shard_map/pallas_call | solution.py:178
  79.8 0.0 copy-start
  79.8 1.0 copy-done
  80.8 0.0 reduce-scatter.2.cloned.1.call-update
  80.8 0.0 copy-start.2
  80.8 1.2 copy-done.2
  82.0 1.9 %shard_map.95 = (bf16[256,384]{1,0:T(8,128)(2,1)S(1)}, bf16[256,384]{1,0:T(8,128)(2,1)S(1)}) custom-call(s32[2]{0:T(128)S(1)} %pad_add_fusion.where_ref, bf16[8,256,256]{2,1,0:T(8,128)(2,1)S(1)} %bitcast.12, bf16[4,4,192,256]{3,2,1,0:T(8,128)(2,1)S(1)} %all-to-all-done.near_w_ref, bf16[4,4,192,256]{3,2,1,0:T(8,128)(2,1)S(1)} %collective-permute-done.4.far_w_ref), custom_call_target="tpu_custom_call" | custom-call | flops 536870912 | bytes 4194304 | tf_op jit(solution)/shard_map/pallas_call | solution.py:182
  83.9 0.0 copy-start.3
  83.9 0.0 copy-start.4
  83.9 0.0 copy-start.5
  84.0 0.0 copy-start.6
  84.0 3.9 %collective-permute-start.5 = (bf16[256,384]{1,0:T(8,128)(2,1)S(1)}, bf16[256,384]{1,0:T(8,128)(2,1)S(1)}, u32[]{:S(2)}, u32[]{:S(2)}) collective-permute-start(bf16[256,384]{1,0:T(8,128)(2,1)S(1)} %get-tuple-element.30), channel_id=1, source_target_pairs={{0,1},{1,0},{2,3},{3,2},{4,5},{5,4},{6,7},{7,6},{8,9},{9,8},{10,11... | collective-permute-start | bytes 589832 | tf_op jit(solution)/shard_map/ppermute | solution.py:143
  87.9 11.7 %all-to-all-done.1.blocks_ref = bf16[4,4,192,256]{3,2,1,0:T(8,128)(2,1)} async-done(((bf16[4,4,192,256]{3,2,1,0:T(8,128)(2,1)}), bf16[4,4,192,256]{3,2,1,0:T(8,128)(2,1)}, u32[]{:S(2)}, u32[]{:S(2)}) %all-to-all-start.1) | async-done | bytes 1572896 | tf_op jit(solution)/shard_map/all_to_all | solution.py:135
  99.6 1.6 %shard_map.96 = bf16[4,192,256]{2,1,0:T(8,128)(2,1)S(1)} custom-call(bf16[4,4,192,256]{3,2,1,0:T(8,128)(2,1)} %all-to-all-done.1.blocks_ref), custom_call_target="tpu_custom_call" | custom-call | flops 1048576 | bytes 2097152 | tf_op jit(solution)/shard_map/pallas_call | solution.py:176
  101.2 0.0 collective-permute-done.5
  101.2 14.7 %all_to_all.15 = bf16[4,192,256]{2,1,0:T(8,128)(2,1)S(1)} all-to-all(bf16[4,192,256]{2,1,0:T(8,128)(2,1)S(1)} %shard_map.96), channel_id=1, replica_groups=mesh['y_lo'=4,'x'=4,'core'=2,'z'=8,'y_hi'=2] {'y_lo'}, dimensions={0} | all-to-all | bytes 786432 | tf_op jit(solution)/shard_map/all_to_all | solution.py:135
  115.9 0.1 fusion
  115.9 7.5 %collective-permute-start.6 = (bf16[192,256]{1,0:T(8,128)(2,1)S(1)}, bf16[192,256]{1,0:T(8,128)(2,1)S(1)}, u32[]{:S(2)}, u32[]{:S(2)}) collective-permute-start(bf16[192,256]{1,0:T(8,128)(2,1)S(1)} %fusion), channel_id=1, source_target_pairs={{0,0},{2,64},{4,128},{6,192},{8,256},{10,320},{12,384},{14,448},{3... | collective-permute-start | bytes 294920 | tf_op jit(solution)/shard_map/ppermute | solution.py:126
  123.4 0.7 add_convert_fusion
  124.1 11.0 %reduce-scatter.2.cloned.1.call-done = bf16[1,256,256]{2,1,0:T(8,128)(2,1)} async-done(((bf16[8,256,256]{2,1,0:T(8,128)(2,1)}), bf16[1,256,256]{2,1,0:T(8,128)(2,1)}) %reduce-scatter.2.cloned.1.call-update) | async-done | bytes 131088 | tf_op jit(solution)/shard_map/reduce_scatter | solution.py:181
  135.1 0.0 copy-done.3
  135.1 0.0 copy-done.4
  135.1 0.0 copy-done.5
  135.1 0.0 copy-done.6
  135.1 0.0 copy-start.8
  135.1 0.9 copy-done.8
  136.0 1.6 %shard_map.98 = (bf16[256,256]{1,0:T(8,128)(2,1)}, bf16[256,256]{1,0:T(8,128)(2,1)}, bf16[256,256]{1,0:T(8,128)(2,1)}) custom-call(bf16[256,256]{1,0:T(8,128)(2,1)S(1)} %copy-done.4, bf16[256,256]{1,0:T(8,128)(2,1)S(1)} %copy-done.5, bf16[256,256]{1,0:T(8,128)(2,1)S(1)} %copy-done.6, f32[2,256,256]{2,1,0:T(8,128)S(1)} %copy-done.3, bf16[256,256]{1,0:T(8,128)(2,1)S(1)} %bitcast.13), custom_call_target="tpu_custom_call" | custom-call | flops 134217728 | bytes 2097152 | tf_op jit(solution)/shard_map/pallas_call | solution.py:197
  137.6 0.0 collective-permute-done.6
  137.6 0.7 convert_bitcast_fusion
Async XLA Ops:
  7.2 51.1 %all-gather.4.cloned.1.call-start = ((), (), s32[]{:S(2)}) async-start(), calls=%async_computation.5 | async-start | bytes 1179648 | tf_op jit(solution)/shard_map/all_gather | solution.py:155
  9.9 20.3 %collective-permute-start = (bf16[192,256]{1,0:T(8,128)(2,1)}, bf16[192,256]{1,0:T(8,128)(2,1)S(1)}, u32[]{:S(2)}, u32[]{:S(2)}) collective-permute-start(bf16[192,256]{1,0:T(8,128)(2,1)} %bitcast.15), channel_id=1, source_target_pairs={{0,0},{2,64},{4,128},{6,192},{8,256},{10,320},{12,384},{14,448},{3... | collective-permute-start | bytes 294920 | tf_op jit(solution)/shard_map/ppermute | solution.py:126
  23.2 25.9 %collective-permute-start.1 = (bf16[256,384]{1,0:T(8,128)(2,1)}, bf16[256,384]{1,0:T(8,128)(2,1)S(1)}, u32[]{:S(2)}, u32[]{:S(2)}) collective-permute-start(bf16[256,384]{1,0:T(8,128)(2,1)} %own_ref), channel_id=1, source_target_pairs={{0,1},{1,0},{2,3},{3,2},{4,5},{5,4},{6,7},{7,6},{8,9},{9,8},{10,11... | collective-permute-start | bytes 589832 | tf_op jit(solution)/shard_map/ppermute | solution.py:143
  50.4 9.9 %copy-start.7 = (bf16[256,384]{1,0:T(8,128)(2,1)S(1)}, bf16[256,384]{1,0:T(8,128)(2,1)}, u32[]{:S(2)}) copy-start(bf16[256,384]{1,0:T(8,128)(2,1)} %own_ref) | copy-start | bytes 589828
  50.4 21.1 %all-to-all-start = ((bf16[4,4,192,256]{3,2,1,0:T(8,128)(2,1)}), bf16[4,4,192,256]{3,2,1,0:T(8,128)(2,1)S(1)}, u32[]{:S(2)}, u32[]{:S(2)}) async-start(bf16[4,4,192,256]{3,2,1,0:T(8,128)(2,1)} %broadcast_in_dim.2), calls=%async_computation | async-start | bytes 3145728 | tf_op jit(solution)/shard_map/all_to_all | solution.py:131
  58.3 6.2 %collective-permute-start.2 = (bf16[8,256,256]{2,1,0:T(8,128)(2,1)}, bf16[8,256,256]{2,1,0:T(8,128)(2,1)S(1)}, u32[]{:S(2)}, u32[]{:S(2)}) collective-permute-start(bf16[8,256,256]{2,1,0:T(8,128)(2,1)} %bitcast.10), channel_id=1, source_target_pairs={{0,16},{16,0},{1,17},{17,1},{2,18},{18,2},{3,19},{19,3},{4,20},{20... | collective-permute-start | bytes 3145736 | tf_op jit(solution)/shard_map/ppermute | solution.py:143
  61.0 3.5 %collective-permute-start.3 = (bf16[384,256]{1,0:T(8,128)(2,1)S(1)}, bf16[384,256]{1,0:T(8,128)(2,1)S(1)}, u32[]{:S(2)}, u32[]{:S(2)}) collective-permute-start(bf16[384,256]{1,0:T(8,128)(2,1)S(1)} %get-tuple-element.27.theirs_ref), channel_id=1, source_target_pairs={{0,16},{16,0},{1,17},{17,1},{2,18},{18,2},{3,19},{19,3},{4,20},{20... | collective-permute-start | bytes 589832 | tf_op jit(solution)/shard_map/ppermute | solution.py:143
  64.5 1.2 copy-start.1
  71.5 6.4 %collective-permute-start.4 = (bf16[4,4,192,256]{3,2,1,0:T(8,128)(2,1)S(1)}, bf16[4,4,192,256]{3,2,1,0:T(8,128)(2,1)S(1)}, u32[]{:S(2)}, u32[]{:S(2)}) collective-permute-start(bf16[4,4,192,256]{3,2,1,0:T(8,128)(2,1)S(1)} %all-to-all-done.near_w_ref), channel_id=1, source_target_pairs={{0,16},{16,0},{1,17},{17,1},{2,18},{18,2},{3,19},{19,3},{4,20},{20... | collective-permute-start | bytes 4718600 | tf_op jit(solution)/shard_map/ppermute | solution.py:143
  73.5 26.1 %all-to-all-start.1 = ((bf16[4,4,192,256]{3,2,1,0:T(8,128)(2,1)}), bf16[4,4,192,256]{3,2,1,0:T(8,128)(2,1)}, u32[]{:S(2)}, u32[]{:S(2)}) async-start(bf16[4,4,192,256]{3,2,1,0:T(8,128)(2,1)} %shard_map.94), calls=%async_computation.1 | async-start | bytes 3145728 | tf_op jit(solution)/shard_map/all_to_all | solution.py:135
  77.9 57.3 %reduce-scatter.2.cloned.1.call-start = ((), (), s32[]{:S(2)}) async-start(), calls=%async_computation.4 | async-start | bytes 1179648 | tf_op jit(solution)/shard_map/reduce_scatter | solution.py:181
  79.8 1.0 copy-start
  80.8 1.2 copy-start.2
  83.9 51.2 %copy-start.3 = (f32[2,256,256]{2,1,0:T(8,128)S(1)}, f32[2,256,256]{2,1,0:T(8,128)}, u32[]{:S(2)}) copy-start(f32[2,256,256]{2,1,0:T(8,128)} %get-tuple-element.33.probs_ref) | copy-start | bytes 1572868
  83.9 51.2 %copy-start.4 = (bf16[256,256]{1,0:T(8,128)(2,1)S(1)}, bf16[256,256]{1,0:T(8,128)(2,1)}, u32[]{:S(2)}) copy-start(bf16[256,256]{1,0:T(8,128)(2,1)} %q_ref.3) | copy-start | bytes 393220
  83.9 51.2 %copy-start.5 = (bf16[256,256]{1,0:T(8,128)(2,1)S(1)}, bf16[256,256]{1,0:T(8,128)(2,1)}, u32[]{:S(2)}) copy-start(bf16[256,256]{1,0:T(8,128)(2,1)} %k_ref.3) | copy-start | bytes 393220
  84.0 51.2 %copy-start.6 = (bf16[256,256]{1,0:T(8,128)(2,1)S(1)}, bf16[256,256]{1,0:T(8,128)(2,1)}, u32[]{:S(2)}) copy-start(bf16[256,256]{1,0:T(8,128)(2,1)} %v_ref.3) | copy-start | bytes 393220
  84.0 17.2 %collective-permute-start.5 = (bf16[256,384]{1,0:T(8,128)(2,1)S(1)}, bf16[256,384]{1,0:T(8,128)(2,1)S(1)}, u32[]{:S(2)}, u32[]{:S(2)}) collective-permute-start(bf16[256,384]{1,0:T(8,128)(2,1)S(1)} %get-tuple-element.30), channel_id=1, source_target_pairs={{0,1},{1,0},{2,3},{3,2},{4,5},{5,4},{6,7},{7,6},{8,9},{9,8},{10,11... | collective-permute-start | bytes 589832 | tf_op jit(solution)/shard_map/ppermute | solution.py:143
  115.9 21.7 %collective-permute-start.6 = (bf16[192,256]{1,0:T(8,128)(2,1)S(1)}, bf16[192,256]{1,0:T(8,128)(2,1)S(1)}, u32[]{:S(2)}, u32[]{:S(2)}) collective-permute-start(bf16[192,256]{1,0:T(8,128)(2,1)S(1)} %fusion), channel_id=1, source_target_pairs={{0,0},{2,64},{4,128},{6,192},{8,256},{10,320},{12,384},{14,448},{3... | collective-permute-start | bytes 294920 | tf_op jit(solution)/shard_map/ppermute | solution.py:126
  135.1 0.9 copy-start.8
Sparse Core Ops, SparseCore 0:
  10.7 47.6 all-gather.3
  81.5 53.5 reduce-scatter.1

commit v5 on v4

--- a/solution.py
+++ b/solution.py
@@ -192,13 +192,13 @@
     received = swap(send, "y_hi")
     layer_out = total([keep, received]).astype(BF16)
     term, received = lax.optimization_barrier((term, received))
-    term = total(scatter(term, "y_lo")).astype(BF16)
+    term = total(scatter(term, "y_lo")).astype(BF16).T
     term = change_plane(term)
     grad_query, grad_key, grad_value = call(
         attend_back, [square] * 3, [], 2**27, 2**21, 5, vmem_mib=6
     )(query_rows, key_rows, value_rows, probs, dctx)
     term, grad_query = lax.optimization_barrier((term, grad_query))
-    grad_weight = term.T.astype(F32)
+    grad_weight = term.astype(F32)
     return (layer_out, grad_query, grad_key, grad_value, grad_weight)
 
 

time: 146 us -> 146 us (level)
  no operation moved by 1% of the time
where the time goes in v5:
time: 146 us; the launch traced here: 145 us
  starting transfers between devices  43.7 us (30%)
  blocking collectives  33.5 us (23%)
  waiting for transfers between devices  33.4 us (23%)
  between operations  14.2 us (10%)
  Pallas kernels  13.1 us (9%)
  local copies, waits for them, and re-layouts  5.67 us (4%)
  other arithmetic  1.55 us (1%)
    ppermute x2, starting transfers between devices, change_plane(): return lax.ppermute(block, ('y_lo', 'x', 'z'), plane_pairs())  20.8 us
    all_gather x1, blocking collectives, local(): weight = lax.all_gather(weight, 'y_lo', axis=0)  18.9 us
    all_to_all x1, blocking collectives, scatter(): return lax.all_to_all(blocks, axis, split_axis=0, concat_axis=0, tiled=True)  14.7 us
    ppermute x5, starting transfers between devices, swap(): return lax.ppermute(block, axis, [(0, 1), (1, 0)])  12.2 us
    all_to_all x1, waiting for transfers between devices, scatter(): return lax.all_to_all(blocks, axis, split_axis=0, concat_axis=0, tiled=True)  11.7 us
    reduce_scatter x1, waiting for transfers between devices, local(): dctx = lax.psum_scatter(dctx, 'z', scatter_dimension=0, tiled=True)[0]  11 us
    all_to_all x1, starting transfers between devices, gather(): return lax.all_to_all(wide, axis, split_axis=0, concat_axis=0, tiled=True)  6.24 us
    ppermute x2, waiting for transfers between devices, change_plane(): return lax.ppermute(block, ('y_lo', 'x', 'z'), plane_pairs())  5 us
  transfers between devices with their start and end apart: 11, of which 6 were waited for; matrix products, arithmetic and copies ran while one was open for 1% of the time, Pallas kernels for 7%

profile of v5, /device:TPU:56, one launch (start us, length us, event | category | flops | bytes accessed | tf_op | source)
XLA Modules:
  0.0 145.2 jit_solution(9847494432941771575)
XLA Ops:
  7.2 0.0 all-gather.4.cloned.1.call-start
  7.2 2.7 %shard_map.92 = (bf16[256,256]{1,0:T(8,128)(2,1)}, f32[2,256,256]{2,1,0:T(8,128)}) custom-call(bf16[256,256]{1,0:T(8,128)(2,1)} %q_ref.3, bf16[256,256]{1,0:T(8,128)(2,1)} %k_ref.3, bf16[256,256]{1,0:T(8,128)(2,1)} %v_ref.3), custom_call_target="tpu_custom_call" | custom-call | flops 67108864 | bytes 1048576 | tf_op jit(solution)/shard_map/pallas_call | solution.py:152
  9.9 0.0 all-gather.4.cloned.1.call-update
  9.9 13.3 %collective-permute-start = (bf16[192,256]{1,0:T(8,128)(2,1)}, bf16[192,256]{1,0:T(8,128)(2,1)S(1)}, u32[]{:S(2)}, u32[]{:S(2)}) collective-permute-start(bf16[192,256]{1,0:T(8,128)(2,1)} %bitcast.15), channel_id=1, source_target_pairs={{0,0},{2,64},{4,128},{6,192},{8,256},{10,320},{12,384},{14,448},{3... | collective-permute-start | bytes 294920 | tf_op jit(solution)/shard_map/ppermute | solution.py:126
  23.2 2.0 %collective-permute-start.1 = (bf16[256,384]{1,0:T(8,128)(2,1)}, bf16[256,384]{1,0:T(8,128)(2,1)S(1)}, u32[]{:S(2)}, u32[]{:S(2)}) collective-permute-start(bf16[256,384]{1,0:T(8,128)(2,1)} %own_ref), channel_id=1, source_target_pairs={{0,1},{1,0},{2,3},{3,2},{4,5},{5,4},{6,7},{7,6},{8,9},{9,8},{10,11... | collective-permute-start | bytes 589832 | tf_op jit(solution)/shard_map/ppermute | solution.py:143
  25.2 5.0 %collective-permute-done = bf16[192,256]{1,0:T(8,128)(2,1)S(1)} collective-permute-done((bf16[192,256]{1,0:T(8,128)(2,1)}, bf16[192,256]{1,0:T(8,128)(2,1)S(1)}, u32[]{:S(2)}, u32[]{:S(2)}) %collective-permute-start) | collective-permute-done | bytes 98336 | tf_op jit(solution)/shard_map/ppermute | solution.py:126
  30.2 18.9 %all-gather.1 = bf16[768,256]{1,0:T(8,128)(2,1)S(1)} all-gather(bf16[192,256]{1,0:T(8,128)(2,1)S(1)} %collective-permute-done), channel_id=3, replica_groups=mesh['y_lo'=4,'x'=4,'core'=2,'z'=8,'y_hi'=2] {'y_lo'}, dimensions={0}, use_global_device_ids=true | all-gather | bytes 491520 | tf_op jit(solution)/shard_map/all_gather | solution.py:160
  49.1 0.0 collective-permute-done.1.far_ref
  49.1 1.3 broadcast_in_dim.2
  50.4 0.0 copy-start.7
  50.4 6.2 %all-to-all-start = ((bf16[4,4,192,256]{3,2,1,0:T(8,128)(2,1)}), bf16[4,4,192,256]{3,2,1,0:T(8,128)(2,1)S(1)}, u32[]{:S(2)}, u32[]{:S(2)}) async-start(bf16[4,4,192,256]{3,2,1,0:T(8,128)(2,1)} %broadcast_in_dim.2), calls=%async_computation | async-start | bytes 3145728 | tf_op jit(solution)/shard_map/all_to_all | solution.py:131
  56.7 1.6 %all-gather.4.cloned.1.call-done = bf16[2048,256]{1,0:T(8,128)(2,1)} async-done(((bf16[256,256]{1,0:T(8,128)(2,1)}), bf16[2048,256]{1,0:T(8,128)(2,1)}) %all-gather.4.cloned.1.call-update) | async-done | bytes 1048592 | tf_op jit(solution)/shard_map/all_gather | solution.py:155
  58.3 1.9 %collective-permute-start.2 = (bf16[8,256,256]{2,1,0:T(8,128)(2,1)}, bf16[8,256,256]{2,1,0:T(8,128)(2,1)S(1)}, u32[]{:S(2)}, u32[]{:S(2)}) collective-permute-start(bf16[8,256,256]{2,1,0:T(8,128)(2,1)} %bitcast.10), channel_id=1, source_target_pairs={{0,16},{16,0},{1,17},{17,1},{2,18},{18,2},{3,19},{19,3},{4,20},{20... | collective-permute-start | bytes 3145736 | tf_op jit(solution)/shard_map/ppermute | solution.py:143
  60.2 0.1 pad_add_fusion.where_ref
  60.3 0.0 copy-done.7
  60.3 0.7 shard_map.93
  61.0 2.4 %collective-permute-start.3 = (bf16[384,256]{1,0:T(8,128)(2,1)S(1)}, bf16[384,256]{1,0:T(8,128)(2,1)S(1)}, u32[]{:S(2)}, u32[]{:S(2)}) collective-permute-start(bf16[384,256]{1,0:T(8,128)(2,1)S(1)} %get-tuple-element.27.theirs_ref), channel_id=1, source_target_pairs={{0,16},{16,0},{1,17},{17,1},{2,18},{18,2},{3,19},{19,3},{4,20},{20... | collective-permute-start | bytes 589832 | tf_op jit(solution)/shard_map/ppermute | solution.py:143
  63.5 1.0 collective-permute-done.3.other_cot_ref
  64.5 0.0 collective-permute-done.2.other_ctx_ref
  64.5 0.0 copy-start.1
  64.5 1.2 copy-done.1
  65.7 2.8 %shard_map.94 = bf16[4,4,192,256]{3,2,1,0:T(8,128)(2,1)} custom-call(s32[2]{0:T(128)S(1)} %pad_add_fusion.where_ref, bf16[8,256,256]{2,1,0:T(8,128)(2,1)S(1)} %bitcast.11, bf16[8,256,256]{2,1,0:T(8,128)(2,1)S(1)} %collective-permute-done.2.other_ctx_ref, bf16[384,256]{1,0:T(8,128)(2,1)S(1)} %get-tuple-element.26.cot_ref.mine_ref, ...), custom_call_target="tpu_custom_call" | custom-call | flops 536870912 | bytes 4194304 | tf_op jit(solution)/shard_map/pallas_call | solution.py:170
  68.5 3.0 %all-to-all-done.near_w_ref = bf16[4,4,192,256]{3,2,1,0:T(8,128)(2,1)S(1)} async-done(((bf16[4,4,192,256]{3,2,1,0:T(8,128)(2,1)}), bf16[4,4,192,256]{3,2,1,0:T(8,128)(2,1)S(1)}, u32[]{:S(2)}, u32[]{:S(2)}) %all-to-all-start) | async-done | bytes 1572896 | tf_op jit(solution)/shard_map/all_to_all | solution.py:131
  71.5 1.9 %collective-permute-start.4 = (bf16[4,4,192,256]{3,2,1,0:T(8,128)(2,1)S(1)}, bf16[4,4,192,256]{3,2,1,0:T(8,128)(2,1)S(1)}, u32[]{:S(2)}, u32[]{:S(2)}) collective-permute-start(bf16[4,4,192,256]{3,2,1,0:T(8,128)(2,1)S(1)} %all-to-all-done.near_w_ref), channel_id=1, source_target_pairs={{0,16},{16,0},{1,17},{17,1},{2,18},{18,2},{3,19},{19,3},{4,20},{20... | collective-permute-start | bytes 4718600 | tf_op jit(solution)/shard_map/ppermute | solution.py:143
  73.5 4.4 %all-to-all-start.1 = ((bf16[4,4,192,256]{3,2,1,0:T(8,128)(2,1)}), bf16[4,4,192,256]{3,2,1,0:T(8,128)(2,1)}, u32[]{:S(2)}, u32[]{:S(2)}) async-start(bf16[4,4,192,256]{3,2,1,0:T(8,128)(2,1)} %shard_map.94), calls=%async_computation.1 | async-start | bytes 3145728 | tf_op jit(solution)/shard_map/all_to_all | solution.py:135
  77.9 0.0 reduce-scatter.2.cloned.1.call-start
  77.9 0.0 collective-permute-done.4.far_w_ref
  77.9 1.9 %shard_map.97 = bf16[8,256,256]{2,1,0:T(8,128)(2,1)S(1)} custom-call(s32[2]{0:T(128)S(1)} %pad_add_fusion.where_ref, bf16[384,256]{1,0:T(8,128)(2,1)S(1)} %get-tuple-element.26.cot_ref.mine_ref, bf16[384,256]{1,0:T(8,128)(2,1)S(1)} %get-tuple-element.27.theirs_ref, bf16[4,4,192,256]{3,2,1,0:T(8,128)(2,1)S(1)} %all-to-all-done.near_w_ref, ...), custom_call_target="tpu_custom_call" | custom-call | flops 536870912 | bytes 4194304 | tf_op jit(solution)/shard_map/pallas_call | solution.py:178
  79.8 0.0 copy-start
  79.8 1.0 copy-done
  80.8 0.0 reduce-scatter.2.cloned.1.call-update
  80.8 0.0 copy-start.2
  80.8 1.2 copy-done.2
  82.0 1.9 %shard_map.95 = (bf16[256,384]{1,0:T(8,128)(2,1)S(1)}, bf16[256,384]{1,0:T(8,128)(2,1)S(1)}) custom-call(s32[2]{0:T(128)S(1)} %pad_add_fusion.where_ref, bf16[8,256,256]{2,1,0:T(8,128)(2,1)S(1)} %bitcast.12, bf16[4,4,192,256]{3,2,1,0:T(8,128)(2,1)S(1)} %all-to-all-done.near_w_ref, bf16[4,4,192,256]{3,2,1,0:T(8,128)(2,1)S(1)} %collective-permute-done.4.far_w_ref), custom_call_target="tpu_custom_call" | custom-call | flops 536870912 | bytes 4194304 | tf_op jit(solution)/shard_map/pallas_call | solution.py:182
  83.9 0.0 copy-start.3
  83.9 0.0 copy-start.4
  83.9 0.0 copy-start.5
  84.0 0.0 copy-start.6
  84.0 3.9 %collective-permute-start.5 = (bf16[256,384]{1,0:T(8,128)(2,1)S(1)}, bf16[256,384]{1,0:T(8,128)(2,1)S(1)}, u32[]{:S(2)}, u32[]{:S(2)}) collective-permute-start(bf16[256,384]{1,0:T(8,128)(2,1)S(1)} %get-tuple-element.30), channel_id=1, source_target_pairs={{0,1},{1,0},{2,3},{3,2},{4,5},{5,4},{6,7},{7,6},{8,9},{9,8},{10,11... | collective-permute-start | bytes 589832 | tf_op jit(solution)/shard_map/ppermute | solution.py:143
  87.9 11.7 %all-to-all-done.1.blocks_ref = bf16[4,4,192,256]{3,2,1,0:T(8,128)(2,1)} async-done(((bf16[4,4,192,256]{3,2,1,0:T(8,128)(2,1)}), bf16[4,4,192,256]{3,2,1,0:T(8,128)(2,1)}, u32[]{:S(2)}, u32[]{:S(2)}) %all-to-all-start.1) | async-done | bytes 1572896 | tf_op jit(solution)/shard_map/all_to_all | solution.py:135
  99.6 1.6 %shard_map.96 = bf16[4,192,256]{2,1,0:T(8,128)(2,1)S(1)} custom-call(bf16[4,4,192,256]{3,2,1,0:T(8,128)(2,1)} %all-to-all-done.1.blocks_ref), custom_call_target="tpu_custom_call" | custom-call | flops 1048576 | bytes 2097152 | tf_op jit(solution)/shard_map/pallas_call | solution.py:176
  101.2 0.0 collective-permute-done.5
  101.2 14.7 %all_to_all.15 = bf16[4,192,256]{2,1,0:T(8,128)(2,1)S(1)} all-to-all(bf16[4,192,256]{2,1,0:T(8,128)(2,1)S(1)} %shard_map.96), channel_id=1, replica_groups=mesh['y_lo'=4,'x'=4,'core'=2,'z'=8,'y_hi'=2] {'y_lo'}, dimensions={0} | all-to-all | bytes 786432 | tf_op jit(solution)/shard_map/all_to_all | solution.py:135
  115.9 0.1 fusion
  115.9 7.5 %collective-permute-start.6 = (bf16[256,192]{0,1:T(8,128)(2,1)S(1)}, bf16[256,192]{0,1:T(8,128)(2,1)S(1)}, u32[]{:S(2)}, u32[]{:S(2)}) collective-permute-start(bf16[256,192]{0,1:T(8,128)(2,1)S(1)} %fusion), channel_id=1, source_target_pairs={{0,0},{2,64},{4,128},{6,192},{8,256},{10,320},{12,384},{14,448},{3... | collective-permute-start | bytes 294920 | tf_op jit(solution)/shard_map/ppermute | solution.py:126
  123.4 0.7 add_convert_fusion
  124.1 11.0 %reduce-scatter.2.cloned.1.call-done = bf16[1,256,256]{2,1,0:T(8,128)(2,1)} async-done(((bf16[8,256,256]{2,1,0:T(8,128)(2,1)}), bf16[1,256,256]{2,1,0:T(8,128)(2,1)}) %reduce-scatter.2.cloned.1.call-update) | async-done | bytes 131088 | tf_op jit(solution)/shard_map/reduce_scatter | solution.py:181
  135.1 0.0 copy-done.3
  135.1 0.0 copy-done.4
  135.1 0.0 copy-done.5
  135.1 0.0 copy-done.6
  135.1 0.0 copy-start.8
  135.1 0.9 copy-done.8
  136.0 1.6 %shard_map.98 = (bf16[256,256]{1,0:T(8,128)(2,1)}, bf16[256,256]{1,0:T(8,128)(2,1)}, bf16[256,256]{1,0:T(8,128)(2,1)}) custom-call(bf16[256,256]{1,0:T(8,128)(2,1)S(1)} %copy-done.4, bf16[256,256]{1,0:T(8,128)(2,1)S(1)} %copy-done.5, bf16[256,256]{1,0:T(8,128)(2,1)S(1)} %copy-done.6, f32[2,256,256]{2,1,0:T(8,128)S(1)} %copy-done.3, bf16[256,256]{1,0:T(8,128)(2,1)S(1)} %bitcast.13), custom_call_target="tpu_custom_call" | custom-call | flops 134217728 | bytes 2097152 | tf_op jit(solution)/shard_map/pallas_call | solution.py:197
  137.6 0.0 collective-permute-done.6
  137.6 0.7 convert_element_type.36
Async XLA Ops:
  7.2 51.1 %all-gather.4.cloned.1.call-start = ((), (), s32[]{:S(2)}) async-start(), calls=%async_computation.5 | async-start | bytes 1179648 | tf_op jit(solution)/shard_map/all_gather | solution.py:155
  9.9 20.3 %collective-permute-start = (bf16[192,256]{1,0:T(8,128)(2,1)}, bf16[192,256]{1,0:T(8,128)(2,1)S(1)}, u32[]{:S(2)}, u32[]{:S(2)}) collective-permute-start(bf16[192,256]{1,0:T(8,128)(2,1)} %bitcast.15), channel_id=1, source_target_pairs={{0,0},{2,64},{4,128},{6,192},{8,256},{10,320},{12,384},{14,448},{3... | collective-permute-start | bytes 294920 | tf_op jit(solution)/shard_map/ppermute | solution.py:126
  23.2 25.9 %collective-permute-start.1 = (bf16[256,384]{1,0:T(8,128)(2,1)}, bf16[256,384]{1,0:T(8,128)(2,1)S(1)}, u32[]{:S(2)}, u32[]{:S(2)}) collective-permute-start(bf16[256,384]{1,0:T(8,128)(2,1)} %own_ref), channel_id=1, source_target_pairs={{0,1},{1,0},{2,3},{3,2},{4,5},{5,4},{6,7},{7,6},{8,9},{9,8},{10,11... | collective-permute-start | bytes 589832 | tf_op jit(solution)/shard_map/ppermute | solution.py:143
  50.4 9.9 %copy-start.7 = (bf16[256,384]{1,0:T(8,128)(2,1)S(1)}, bf16[256,384]{1,0:T(8,128)(2,1)}, u32[]{:S(2)}) copy-start(bf16[256,384]{1,0:T(8,128)(2,1)} %own_ref) | copy-start | bytes 589828
  50.4 21.1 %all-to-all-start = ((bf16[4,4,192,256]{3,2,1,0:T(8,128)(2,1)}), bf16[4,4,192,256]{3,2,1,0:T(8,128)(2,1)S(1)}, u32[]{:S(2)}, u32[]{:S(2)}) async-start(bf16[4,4,192,256]{3,2,1,0:T(8,128)(2,1)} %broadcast_in_dim.2), calls=%async_computation | async-start | bytes 3145728 | tf_op jit(solution)/shard_map/all_to_all | solution.py:131
  58.3 6.2 %collective-permute-start.2 = (bf16[8,256,256]{2,1,0:T(8,128)(2,1)}, bf16[8,256,256]{2,1,0:T(8,128)(2,1)S(1)}, u32[]{:S(2)}, u32[]{:S(2)}) collective-permute-start(bf16[8,256,256]{2,1,0:T(8,128)(2,1)} %bitcast.10), channel_id=1, source_target_pairs={{0,16},{16,0},{1,17},{17,1},{2,18},{18,2},{3,19},{19,3},{4,20},{20... | collective-permute-start | bytes 3145736 | tf_op jit(solution)/shard_map/ppermute | solution.py:143
  61.0 3.5 %collective-permute-start.3 = (bf16[384,256]{1,0:T(8,128)(2,1)S(1)}, bf16[384,256]{1,0:T(8,128)(2,1)S(1)}, u32[]{:S(2)}, u32[]{:S(2)}) collective-permute-start(bf16[384,256]{1,0:T(8,128)(2,1)S(1)} %get-tuple-element.27.theirs_ref), channel_id=1, source_target_pairs={{0,16},{16,0},{1,17},{17,1},{2,18},{18,2},{3,19},{19,3},{4,20},{20... | collective-permute-start | bytes 589832 | tf_op jit(solution)/shard_map/ppermute | solution.py:143
  64.5 1.2 copy-start.1
  71.5 6.4 %collective-permute-start.4 = (bf16[4,4,192,256]{3,2,1,0:T(8,128)(2,1)S(1)}, bf16[4,4,192,256]{3,2,1,0:T(8,128)(2,1)S(1)}, u32[]{:S(2)}, u32[]{:S(2)}) collective-permute-start(bf16[4,4,192,256]{3,2,1,0:T(8,128)(2,1)S(1)} %all-to-all-done.near_w_ref), channel_id=1, source_target_pairs={{0,16},{16,0},{1,17},{17,1},{2,18},{18,2},{3,19},{19,3},{4,20},{20... | collective-permute-start | bytes 4718600 | tf_op jit(solution)/shard_map/ppermute | solution.py:143
  73.5 26.1 %all-to-all-start.1 = ((bf16[4,4,192,256]{3,2,1,0:T(8,128)(2,1)}), bf16[4,4,192,256]{3,2,1,0:T(8,128)(2,1)}, u32[]{:S(2)}, u32[]{:S(2)}) async-start(bf16[4,4,192,256]{3,2,1,0:T(8,128)(2,1)} %shard_map.94), calls=%async_computation.1 | async-start | bytes 3145728 | tf_op jit(solution)/shard_map/all_to_all | solution.py:135
  77.9 57.3 %reduce-scatter.2.cloned.1.call-start = ((), (), s32[]{:S(2)}) async-start(), calls=%async_computation.4 | async-start | bytes 1179648 | tf_op jit(solution)/shard_map/reduce_scatter | solution.py:181
  79.8 1.0 copy-start
  80.8 1.2 copy-start.2
  83.9 51.2 %copy-start.3 = (f32[2,256,256]{2,1,0:T(8,128)S(1)}, f32[2,256,256]{2,1,0:T(8,128)}, u32[]{:S(2)}) copy-start(f32[2,256,256]{2,1,0:T(8,128)} %get-tuple-element.33.probs_ref) | copy-start | bytes 1572868
  83.9 51.2 %copy-start.4 = (bf16[256,256]{1,0:T(8,128)(2,1)S(1)}, bf16[256,256]{1,0:T(8,128)(2,1)}, u32[]{:S(2)}) copy-start(bf16[256,256]{1,0:T(8,128)(2,1)} %q_ref.3) | copy-start | bytes 393220
  83.9 51.2 %copy-start.5 = (bf16[256,256]{1,0:T(8,128)(2,1)S(1)}, bf16[256,256]{1,0:T(8,128)(2,1)}, u32[]{:S(2)}) copy-start(bf16[256,256]{1,0:T(8,128)(2,1)} %k_ref.3) | copy-start | bytes 393220
  84.0 51.2 %copy-start.6 = (bf16[256,256]{1,0:T(8,128)(2,1)S(1)}, bf16[256,256]{1,0:T(8,128)(2,1)}, u32[]{:S(2)}) copy-start(bf16[256,256]{1,0:T(8,128)(2,1)} %v_ref.3) | copy-start | bytes 393220
  84.0 17.2 %collective-permute-start.5 = (bf16[256,384]{1,0:T(8,128)(2,1)S(1)}, bf16[256,384]{1,0:T(8,128)(2,1)S(1)}, u32[]{:S(2)}, u32[]{:S(2)}) collective-permute-start(bf16[256,384]{1,0:T(8,128)(2,1)S(1)} %get-tuple-element.30), channel_id=1, source_target_pairs={{0,1},{1,0},{2,3},{3,2},{4,5},{5,4},{6,7},{7,6},{8,9},{9,8},{10,11... | collective-permute-start | bytes 589832 | tf_op jit(solution)/shard_map/ppermute | solution.py:143
  115.9 21.7 %collective-permute-start.6 = (bf16[256,192]{0,1:T(8,128)(2,1)S(1)}, bf16[256,192]{0,1:T(8,128)(2,1)S(1)}, u32[]{:S(2)}, u32[]{:S(2)}) collective-permute-start(bf16[256,192]{0,1:T(8,128)(2,1)S(1)} %fusion), channel_id=1, source_target_pairs={{0,0},{2,64},{4,128},{6,192},{8,256},{10,320},{12,384},{14,448},{3... | collective-permute-start | bytes 294920 | tf_op jit(solution)/shard_map/ppermute | solution.py:126
  135.1 0.9 copy-start.8
Sparse Core Ops, SparseCore 0:
  10.7 47.6 all-gather.3
  81.5 53.5 reduce-scatter.1
